TPU v7x, 32 devices: a whole 2x2x4 slice. The times are simulated.
32 devices in a mesh: row: 4 (over z), col: 8 (over y, x, core).
Axes of the slice: x: 2, y: 2, z: 4, core: 2. Of those that a mesh axis runs over, the one named last changes fastest.
Arguments:
- t2_amps: bfloat16 [8192, 2048], P('row', 'col'), may hold values from -6 to 6
- v_ints: bfloat16 [2048, 16384], P('row', 'col'), may hold values from -0.125 to 0.125
- t2_mask: int32 [64, 16], P('row', 'col'), may hold values 0 or 1
- v_mask: int32 [16, 128], P('row', 'col'), may hold values 0 or 1
Outputs:
- ladder: bfloat16 [8192, 16384], P('row', 'col')
All inputs are finite; a program needn't handle non-finite values. No bound on the sum of `t2_mask` or of `v_mask` on one device may be relied on, other than what follows from the above.
Results may differ from a plain program's by a relative error of at most 0.001.
Values may be sent and summed in bfloat16 or wider, within the bound.
No kernel may reach another device: no remote copies, remote signals or barrier semaphores. Data moves between devices by JAX's collectives and lax.ppermute only.
A program may use at most 64 MiB of HBM per device.

v0:
```python
import jax
import jax.numpy as jnp
from jax import lax
from jax.sharding import PartitionSpec as P

TILE = 128


def expand(mask, rows, cols):
    kept = jnp.broadcast_to(mask[:, None, :, None] > 0, (mask.shape[0], TILE, mask.shape[1], TILE))
    return kept.reshape(rows, cols)


def body(t2_amps, v_ints, t2_mask, v_mask):
    masked_t2 = jnp.where(
        expand(t2_mask, t2_amps.shape[0], t2_amps.shape[1]), t2_amps, jnp.zeros_like(t2_amps)
    )
    masked_v = jnp.where(
        expand(v_mask, v_ints.shape[0], v_ints.shape[1]), v_ints, jnp.zeros_like(v_ints)
    )
    amp_whole = lax.all_gather(masked_t2, "col", axis=1, tiled=True)
    result = jnp.dot(
        amp_whole,
        lax.all_gather(masked_v, "row", axis=0, tiled=True),
        preferred_element_type=jnp.float32,
    )
    return result.astype(jnp.bfloat16)


def solution(mesh):
    in_specs = (P("row", "col"), P("row", "col"), P("row", "col"), P("row", "col"))
    out_specs = P("row", "col")
    return jax.shard_map(body, mesh=mesh, in_specs=in_specs, out_specs=out_specs, check_vma=False)
```

profile of v0, /device:TPU:0, one launch (start us, length us, event | category | flops | bytes accessed | tf_op | source)
XLA Modules:
  0.0 248.7 jit_solution(16098453369059072586)
XLA Ops:
  6.5 0.0 copy-start
  6.5 0.0 copy-start.1
  6.5 0.0 all-gather.5.cloned.1.call-start
  6.5 0.8 broadcast_compare_fusion
  7.3 0.3 broadcast_in_dim.20
  7.7 3.5 %bitcast_select_fusion = bf16[512,2048]{1,0:T(8,128)(2,1)} fusion(bf16[512,2048]{1,0:T(8,128)(2,1)} %param.5, pred[64,8,16,128]{3,2,1,0:T(8,128)(4,1)S(1)} %bitcast.12), kind=kLoop, calls=%fused_computation.1 | loop fusion | flops 1048576 | bytes 5242880 | tf_op jit(solution)/shard_map/jit(_where)/select_n | solution.py:18
  11.1 0.0 all-gather.5.cloned.1.call-update
  11.1 0.0 all-gather.3.cloned.1.call-start
  11.2 0.0 copy-done
  11.2 0.6 copy.6
  11.9 0.0 copy-done.1
  11.9 0.2 broadcast_in_dim.8
  12.1 1.2 bitcast_select_fusion.1
  13.3 0.0 all-gather.3.cloned.1.call-update
  13.4 150.3 %all-gather.5.cloned.1.call-done = bf16[2048,2048]{1,0:T(8,128)(2,1)} async-done(((bf16[512,2048]{1,0:T(8,128)(2,1)}), bf16[2048,2048]{1,0:T(8,128)(2,1)}) %all-gather.5.cloned.1.call-update) | async-done | bytes 8388624 | tf_op jit(solution)/shard_map/all_gather | solution.py:24
  163.6 54.5 %all-gather.3.cloned.1.call-done = bf16[2048,2048]{0,1:T(8,128)(2,1)} async-done(((bf16[2048,256]{0,1:T(8,128)(2,1)}), bf16[2048,2048]{0,1:T(8,128)(2,1)}) %all-gather.3.cloned.1.call-update) | async-done | bytes 8388624 | tf_op jit(solution)/shard_map/all_gather | solution.py:21
  218.2 23.7 %convolution_convert_fusion = bf16[2048,2048]{1,0:T(8,128)(2,1)} fusion(bf16[2048,2048]{0,1:T(8,128)(2,1)} %all-gather.3.cloned.1.call-done, bf16[2048,2048]{1,0:T(8,128)(2,1)} %all-gather.5.cloned.1.call-done), kind=kOutput, calls=%fused_computation | convolution fusion | flops 17184063488 | bytes 25165824 | tf_op jit(solution)/shard_map/dot_general | solution.py:22
  (1 shorter events, 0.0 us)
Async XLA Ops:
  6.5 4.7 %copy-start = (bf16[2048,256]{1,0:T(8,128)(2,1)S(1)}, bf16[2048,256]{1,0:T(8,128)(2,1)}, u32[]{:S(2)}) copy-start(bf16[2048,256]{1,0:T(8,128)(2,1)} %param.4) | copy-start | bytes 3145732
  6.5 5.3 %copy-start.1 = (s32[16,2]{0,1:T(2,128)S(1)}, s32[16,2]{0,1:T(2,128)}, u32[]{:S(2)}) copy-start(s32[16,2]{0,1:T(2,128)} %param.6) | copy-start | bytes 388
  6.5 157.1 %all-gather.5.cloned.1.call-start = ((), (), s32[]{:S(2)}) async-start(), calls=%async_computation.1 | async-start | bytes 10485760 | tf_op jit(solution)/shard_map/all_gather | solution.py:24
  11.1 207.0 %all-gather.3.cloned.1.call-start = ((), (), s32[]{:S(2)}) async-start(), calls=%async_computation | async-start | bytes 9437184 | tf_op jit(solution)/shard_map/all_gather | solution.py:21
Sparse Core Ops, SparseCore 0:
  11.3 152.3 all-gather.4
  165.5 52.6 all-gather.2
where the time goes:
time: 249 us
  waiting for transfers between devices  205 us (82%)
  matrix products  23.7 us (10%)
  between operations  13.4 us (5%)
  other arithmetic  5.48 us (2%)
    all_gather x1, waiting for transfers between devices, body(): lax.all_gather(masked_v, 'row', axis=0, tiled=True)  150 us
    all_gather x1, waiting for transfers between devices, body(): amp_whole = lax.all_gather(masked_t2, 'col', axis=1, tiled=True)  54.5 us
    dot_general x1, matrix products, body(): jnp.dot(amp_whole, lax.all_gather(masked_v, 'row', axis=0, tiled=True), p...  23.7 us
  transfers between devices with their start and end apart: 2, of which 2 were waited for; matrix products, arithmetic and copies ran while one was open for 1% of the time, Pallas kernels for 0%

commit v1 on v0

v1 whole, which is shorter than its diff:
```python
import functools

import jax
import jax.numpy as jnp
from jax import lax
from jax.experimental import pallas as pl
from jax.experimental.pallas import tpu as pltpu
from jax.sharding import PartitionSpec as P

TILE = 128
PAIR = 2 * TILE
NOTE = 16
BF16 = jnp.bfloat16
LEFTS = 6
SMEM = pl.BlockSpec(memory_space=pltpu.SMEM)
VMEM = pl.BlockSpec(memory_space=pltpu.VMEM)
ANY = pl.BlockSpec(memory_space=pl.ANY)
HBM = pl.BlockSpec(memory_space=pltpu.HBM)
PARAMS = pltpu.CompilerParams(vmem_limit_bytes=48 << 20)
COST = pl.CostEstimate(flops=1 << 20, bytes_accessed=1 << 12, transcendentals=0)
LENGTHS = (8, 10, 12, 14, 16, 20)
FIRST = 28


def rows(tile, count=1):
    return pl.ds(pl.multiple_of(tile * TILE, TILE), count * TILE)


def tiles(count):
    return jax.ShapeDtypeStruct((count * TILE, TILE), BF16)


class Sizes:
    def __init__(self, n, k_tiles, n_tiles):
        self.n, self.kd, self.nd = n, k_tiles, n_tiles
        self.all = k_tiles * n_tiles
        self.main = self.all * 3 // 4
        self.first = self.main * FIRST // 48
        self.left = self.all - self.main
        self.stream = (n - 1) * self.left
        self.pairs = n_tiles // 2
        self.sure = (self.main // k_tiles) // 2
        lengths = {-(-f * self.stream // 48) for f in LENGTHS}
        self.lengths = sorted(lengths | {self.stream})

    def cut(self, c):
        start, stop = ((0, self.first), (self.first, self.main))[c]
        begin = NOTE + start * TILE if c else 0
        return start, stop - start, pl.ds(begin, NOTE + stop * TILE - begin)


def begin_kernel(
    sz, mask_v, v_mask_hbm, t2_mask_hbm, v, t2, main, lf, t2_out,
    v_v, t2_v, packed, v_mask, t2_mask, note, v_sem, sem,
):
    group = sz.nd // v_sem.shape[0]
    copies = []
    for g in range(v_sem.shape[0]):
        at = pl.ds(g * group * TILE, group * TILE)
        copies.append(pltpu.make_async_copy(v.at[:, at], v_v.at[:, at], v_sem.at[g]))
    mask_copy = pltpu.make_async_copy(v_mask_hbm, v_mask, sem.at[0])
    t2_copies = (
        pltpu.make_async_copy(t2_mask_hbm, t2_mask, sem.at[1]),
        pltpu.make_async_copy(t2, t2_v, sem.at[2]),
    )
    for copy in (mask_copy, *copies, *t2_copies):
        copy.start()
    note[...] = jnp.zeros_like(note)
    note[: sz.kd, : sz.nd] = (mask_v[...] > 0).astype(jnp.int32)
    mask_copy.wait()
    pos = jnp.int32(0)
    for c in range(sz.nd):
        if c % group == 0:
            copies[c // group].wait()
        for k in range(sz.kd):
            packed[rows(pos), :] = v_v[k * TILE : (k + 1) * TILE, c * TILE : (c + 1) * TILE]
            pos = pos + (v_mask[k, c] > 0).astype(jnp.int32)
    main[:NOTE, :] = note[...].astype(BF16)
    main[NOTE:, :] = packed[: sz.main * TILE, :]
    lf[...] = packed[sz.main * TILE :, :]
    for copy in t2_copies:
        copy.wait()
    for k in range(t2_mask.shape[0]):
        for i in range(t2_mask.shape[1]):
            at = (slice(i * TILE, (i + 1) * TILE), slice(k * TILE, (k + 1) * TILE))
            tile = t2_v[at]
            t2_out[at] = jnp.where(t2_mask[k, i] > 0, tile, jnp.zeros_like(tile))


def begin(sz, v, t2, v_mask, t2_mask):
    groups = 4 if sz.nd % 4 == 0 else 1
    return pl.pallas_call(
        functools.partial(begin_kernel, sz),
        out_shape=(
            jax.ShapeDtypeStruct((NOTE + sz.main * TILE, TILE), BF16),
            tiles(sz.left),
            jax.ShapeDtypeStruct(t2.shape, BF16),
        ),
        in_specs=[VMEM, HBM, HBM, HBM, HBM],
        out_specs=(VMEM, VMEM, VMEM),
        scratch_shapes=[
            pltpu.VMEM(v.shape, BF16),
            pltpu.VMEM(t2.shape, BF16),
            pltpu.VMEM((sz.all * TILE, TILE), BF16),
            pltpu.SMEM(v_mask.shape, jnp.int32),
            pltpu.SMEM(t2_mask.shape[::-1], jnp.int32),
            pltpu.VMEM((NOTE, TILE), jnp.int32),
            pltpu.SemaphoreType.DMA((groups,)),
            pltpu.SemaphoreType.DMA((3,)),
        ],
        compiler_params=pltpu.CompilerParams(vmem_limit_bytes=60 << 20),
        name="begin",
    )(v_mask, v_mask, t2_mask.T, v, t2)


def need_kernel(sz, here, *refs):
    n = sz.n
    parts, (out, notes, sem) = refs[: 2 * n - 3], refs[2 * n - 3 :]
    copies = [
        pltpu.make_async_copy(ref.at[pl.ds(0, NOTE), :], notes.at[i], sem.at[i])
        for i, ref in enumerate(parts)
    ]
    for copy in copies:
        copy.start()
    for copy in copies:
        copy.wait()
    me = here[0]
    sources = [me]
    for s in range(n - 2):
        sources += [me - 1 - s, me + 1 + s]
    to_up = to_down = jnp.int32(0)
    for i, z in enumerate(sources):
        count = jnp.sum(notes[i].astype(jnp.float32)).astype(jnp.int32)
        left = jnp.where(jnp.logical_and(z >= 0, z < n), jnp.maximum(count - sz.main, 0), 0)
        to_up = to_up + jnp.where(z == n - 1, 0, left)
        to_down = to_down + jnp.where(z == 0, 0, left)
    out[0] = jnp.maximum(to_up, to_down)


def longest(sz, here, own, got):
    ops = (own, *(part for hop in got for part in hop))
    return pl.pallas_call(
        functools.partial(need_kernel, sz),
        out_shape=jax.ShapeDtypeStruct((1,), jnp.int32),
        in_specs=[SMEM] + [ANY] * len(ops),
        out_specs=SMEM,
        scratch_shapes=[
            pltpu.VMEM((len(ops), NOTE, TILE), BF16),
            pltpu.SemaphoreType.DMA((len(ops),)),
        ],
        name="longest",
    )(here, *ops)


def from_source(sz, me, own, got, act):
    for m in range(sz.n):

        @pl.when(me == m)
        def _():
            for z in range(sz.n):
                act(z, own if z == m else got[abs(z - m) - 1][0 if z < m else 1])


def plan_kernel(sz, here, *refs):
    n, me = sz.n, here[0]
    own, *parts, end = refs[: 2 * n - 2]
    place, late, info, notes, wide, masks, note_sem, mask_sem = refs[2 * n - 2 :]

    def note_copy(z, ref):
        at = ref.at[pl.ds(0, NOTE), :]
        return pltpu.make_async_copy(at, notes.at[pl.ds(z * NOTE, NOTE), :], note_sem.at[z])

    got = [parts[2 * s : 2 * s + 2] for s in range(n - 2)] + [(end, end)]
    from_source(sz, me, own, got, lambda z, ref: note_copy(z, ref).start())
    for z in range(n):
        note_copy(z, own).wait()
    wide[...] = notes[...].astype(jnp.int32)
    mask_copy = pltpu.make_async_copy(wide, masks, mask_sem)
    mask_copy.start()
    mask_copy.wait()

    def column(c, carry):
        counts, firsts, seconds = (list(carry[i * n : (i + 1) * n]) for i in range(3))
        for z in range(n):
            have = jnp.where(me == z, sz.all, sz.main)
            for k in range(sz.kd):
                i = c * n * sz.kd + z * sz.kd + k
                kept, p = masks[z * NOTE + k, c] > 0, counts[z]
                place[i] = jnp.where(jnp.logical_and(kept, p < have), z * sz.all + p, n * sz.all)
                late[i] = jnp.where(jnp.logical_and(kept, p >= have), p - sz.main, -1)
                over = jnp.logical_and(kept, p >= sz.first)
                firsts[z] = jnp.where(over, jnp.minimum(firsts[z], c), firsts[z])
                over = jnp.logical_and(kept, p >= have)
                seconds[z] = jnp.where(over, jnp.minimum(seconds[z], c), seconds[z])
                counts[z] = p + kept.astype(jnp.int32)
        return tuple(counts + firsts + seconds)

    start = (jnp.int32(0),) * n + (jnp.int32(sz.nd),) * (2 * n)
    out = lax.fori_loop(0, sz.nd, column, start)
    lefts = [jnp.maximum(c - sz.main, 0) for c in out[:n]]
    info[0] = me
    info[1] = jnp.int32(0)
    info[2] = functools.reduce(jnp.minimum, out[n : 2 * n], jnp.int32(sz.nd - 2)) // 2
    info[3] = functools.reduce(jnp.minimum, out[2 * n :], jnp.int32(sz.nd - 2)) // 2
    info[4] = jnp.int32(sz.pairs)
    info[5] = here[1]
    for z in range(n):
        info[LEFTS + z] = lefts[z]


def plan(sz, here, own, got, end):
    n, ops = sz.n, (own, *(part for hop in got for part in hop), end)
    return pl.pallas_call(
        functools.partial(plan_kernel, sz),
        out_shape=(
            jax.ShapeDtypeStruct((sz.n * sz.all,), jnp.int32),
            jax.ShapeDtypeStruct((sz.n * sz.all,), jnp.int32),
            jax.ShapeDtypeStruct((LEFTS + sz.n,), jnp.int32),
        ),
        in_specs=[SMEM] + [ANY] * len(ops),
        out_specs=(SMEM, SMEM, SMEM),
        scratch_shapes=[
            pltpu.VMEM((n * NOTE, TILE), BF16),
            pltpu.VMEM((n * NOTE, TILE), jnp.int32),
            pltpu.SMEM((n * NOTE, TILE), jnp.int32),
            pltpu.SemaphoreType.DMA((n,)),
            pltpu.SemaphoreType.DMA,
        ],
        name="plan",
    )(here, *ops)


def choose_kernel(sz, c, here, up, down, out, sem):
    at = sz.cut(c)[2]
    for mine, x in ((here[0] == sz.n - 2, up), (here[0] != sz.n - 2, down)):

        @pl.when(mine)
        def _():
            copy = pltpu.make_async_copy(x.at[at, :], out, sem)
            copy.start()
            copy.wait()


def choose(sz, c, here, up, down):
    return pl.pallas_call(
        functools.partial(choose_kernel, sz, c),
        out_shape=jax.ShapeDtypeStruct((sz.cut(c)[2].size, TILE), BF16),
        in_specs=[SMEM, ANY, ANY],
        out_specs=VMEM,
        scratch_shapes=[pltpu.SemaphoreType.DMA],
        compiler_params=PARAMS,
        name="choose",
    )(here, up, down)


def pool_kernel(sz, length, info, lf, *refs):
    n, me = sz.n, info[0]
    spread, (out, joined) = refs[: n - 1], refs[n - 1 :]
    for source, order in ((n - 2, range(n - 2, -1, -1)), (1, range(1, n))):

        @pl.when(me == source)
        def _():
            at = jnp.int32(0)
            for z in order:
                part = lf if z == source else spread[(z ^ source) - 1]
                joined[rows(at, sz.left), :] = part[...]
                at = at + info[LEFTS + z]
            out[...] = joined[: length * TILE, :]


def pool(sz, length, info, lf, spread):
    return pl.pallas_call(
        functools.partial(pool_kernel, sz, length),
        out_shape=tiles(length),
        in_specs=[SMEM] + [VMEM] * sz.n,
        out_specs=VMEM,
        scratch_shapes=[pltpu.VMEM((sz.stream * TILE, TILE), BF16)],
        compiler_params=PARAMS,
        name="pool",
    )(info, lf, *spread)


def out_copy(out, held, sem, slot, pair):
    return pltpu.make_async_copy(
        held.at[slot], out.at[:, pl.ds(pl.multiple_of(pair * PAIR, PAIR), PAIR)], sem.at[slot]
    )


def t2_copies(info, t2, t2_v, sem, r):
    half, wide = t2_v.shape[0] // 2, t2_v.shape[1] // len(t2)
    at = pl.ds(pl.multiple_of(r * half, half), half)
    for d, block in enumerate(t2):
        to = t2_v.at[at, pl.ds(pl.multiple_of((info[5] ^ d) * wide, wide), wide)]
        yield pltpu.make_async_copy(block.at[at, :], to, sem.at[d, r])


def multiply(lo, hi, build, info, t2, t2_v, t2_sem, out, held, sem):
    half = held.shape[1] // 2

    @pl.when(lo >= hi)
    def _():
        for r in range(2):
            for copy in t2_copies(info, t2, t2_v, t2_sem, r):
                copy.wait()

    @pl.loop(lo, hi)
    def _(pair):
        slot = lax.rem(pair - lo, 2)
        b = build(pair)

        @pl.when(pair >= lo + 2)
        def _():
            out_copy(out, held, sem, slot, pair).wait()

        @pl.loop(0, 2)
        def _(r):
            @pl.when(pair == lo)
            def _():
                for copy in t2_copies(info, t2, t2_v, t2_sem, r):
                    copy.wait()

            at = pl.ds(pl.multiple_of(r * half, half), half)
            held[slot, at, :] = jnp.dot(
                t2_v[at, :], b[...], preferred_element_type=jnp.float32
            ).astype(BF16)

        out_copy(out, held, sem, slot, pair).start()

    for back in (1, 2):

        @pl.when(hi - back >= lo)
        def _():
            out_copy(out, held, sem, lax.rem(hi - back - lo, 2), 0).wait()


def main_kernel(sz, chunks, n_t2, info, place, *refs):
    n = sz.n
    t2, refs = refs[:n_t2], refs[n_t2:]
    own, refs = refs[0], refs[1:]
    got, refs = [refs[2 * s : 2 * s + 2] for s in range(n - 2)], refs[2 * (n - 2) :]
    ends, refs = refs[:chunks], refs[chunks:]
    if chunks == 2:
        lf, begun, out, rest, packed, b, held, t2_v, in_sem, out_sem, t2_sem = refs
    else:
        out, packed, b, held, t2_v, in_sem, out_sem, t2_sem = refs
    me = info[0]

    def chunk_copy(ref, z, c):
        start, count, at = sz.cut(c)
        size = count * TILE
        first = at.start + at.size - size if ref.shape[0] > at.size else ref.shape[0] - size
        to = packed.at[pl.ds((z * sz.all + start) * TILE, size), :]
        return pltpu.make_async_copy(ref.at[pl.ds(first, size), :], to, in_sem.at[z, c])

    for c in range(chunks):
        parts = got + [(ends[c], ends[c])]
        from_source(sz, me, own, parts, lambda z, ref: chunk_copy(ref, z, c).start())
    if chunks == 2:
        left_copy = pltpu.make_async_copy(
            lf, packed.at[rows(me * sz.all + sz.main, sz.left), :], in_sem.at[0, 2]
        )
        left_copy.start()
    for r in range(2):
        for copy in t2_copies(info, t2, t2_v, t2_sem, r):
            copy.start()
    packed[n * sz.all * TILE :, :] = jnp.zeros((TILE, TILE), BF16)
    for z in range(n):
        for c in range(chunks):
            chunk_copy(own, z, c).wait()
    if chunks == 2:
        left_copy.wait()

    def build(pair, to=b):
        @pl.loop(0, n * sz.kd)
        def _(k):
            for c in range(2):
                tile = packed[rows(place[(2 * pair + c) * n * sz.kd + k]), :]
                to[rows(k), c * TILE : (c + 1) * TILE] = tile

        return to

    multiply(info[chunks], info[chunks + 1], build, info, t2, t2_v, t2_sem, out, held, out_sem)
    if chunks == 2:
        for j in range(sz.pairs - sz.sure):
            build(sz.sure + j, rest.at[j])


def main_part(sz, chunks, info, place, t2, own, got, ends, lf=None, begun=None):
    ij, cd = t2[0].shape[0], t2[0].shape[1] * len(t2)
    ops = [*t2, own, *(part for hop in got for part in hop), *ends[:chunks]]
    out_shape = [pltpu.HBM((ij, sz.nd * TILE), BF16)]
    aliases = {}
    if chunks == 2:
        ops += [lf, begun]
        aliases = {2 + len(ops) - 1: 0}
        out_shape.append(jax.ShapeDtypeStruct((sz.pairs - sz.sure, cd, PAIR), BF16))
    out = pl.pallas_call(
        functools.partial(main_kernel, sz, chunks, len(t2)),
        out_shape=out_shape,
        in_specs=[SMEM, SMEM] + [ANY] * len(ops),
        out_specs=[HBM, VMEM][:chunks],
        scratch_shapes=[
            pltpu.VMEM(((sz.n * sz.all + 1) * TILE, TILE), BF16),
            pltpu.VMEM((cd, PAIR), BF16),
            pltpu.VMEM((2, ij, PAIR), BF16),
            pltpu.VMEM((ij, cd), BF16),
            pltpu.SemaphoreType.DMA((sz.n, 3)),
            pltpu.SemaphoreType.DMA((2,)),
            pltpu.SemaphoreType.DMA((len(t2), 2)),
        ],
        input_output_aliases=aliases,
        compiler_params=PARAMS,
        cost_estimate=COST,
        name="main_part",
    )(info, place, *ops)
    return out if chunks == 2 else out[0]


def tail_kernel(sz, n_t2, info, late, begun, rest, *refs):
    n, me = sz.n, info[0]
    t2, (top_end, low_end, *refs) = refs[:n_t2], refs[n_t2:]
    spread, (out, b, extra, held, t2_v, in_sem, out_sem, t2_sem) = refs[: n - 1], refs[n - 1 :]
    is_end = jnp.logical_or(me == 0, me == n - 1)
    size = sz.left * TILE
    from_top, from_low = (
        [pltpu.make_async_copy(end, extra.at[pl.ds(0, end.shape[0]), :], in_sem.at[0])]
        for end in (top_end, low_end)
    )
    direct = [
        pltpu.make_async_copy(part, extra.at[pl.ds(i * size, size), :], in_sem.at[i])
        for i, part in enumerate(spread)
    ]

    def each(act):
        for which, copies in ((me == n - 1, from_top), (me == 0, from_low), (jnp.logical_not(is_end), direct)):

            @pl.when(which)
            def _():
                for copy in copies:
                    act(copy)

    each(lambda copy: copy.start())
    for r in range(2):
        for copy in t2_copies(info, t2, t2_v, t2_sem, r):
            copy.start()
    b[...] = rest[...]
    bases = []
    for z in range(n):
        top = sum((info[LEFTS + y] for y in range(z + 1, n - 1)), jnp.int32(0))
        bottom = sum((info[LEFTS + y] for y in range(1, z)), jnp.int32(0))
        base = jnp.where(is_end, jnp.where(me == 0, bottom, top), ((me ^ z) - 1) * sz.left)
        bases.append(base)

    each(lambda copy: copy.wait())
    for j in range(sz.pairs - sz.sure):
        for z in range(n):

            @pl.loop(0, sz.kd)
            def _(k):
                for c in range(2):
                    p = late[((2 * (sz.sure + j) + c) * n + z) * sz.kd + k]

                    @pl.when(p >= 0)
                    def _():
                        b[j, rows(z * sz.kd + k), c * TILE : (c + 1) * TILE] = extra[
                            rows(bases[z] + p), :
                        ]

    multiply(info[3], info[4], lambda pair: b.at[pair - sz.sure], info, t2, t2_v, t2_sem, out, held, out_sem)


def tail_part(sz, info, late, t2, begun, rest, ends, spread):
    ij, cd = t2[0].shape[0], t2[0].shape[1] * len(t2)
    pairs = sz.pairs - sz.sure
    region = max(ends[0].shape[0], (sz.n - 1) * sz.left * TILE)
    return pl.pallas_call(
        functools.partial(tail_kernel, sz, len(t2)),
        out_shape=pltpu.HBM(begun.shape, BF16),
        in_specs=[SMEM, SMEM, HBM, VMEM] + [ANY] * (len(t2) + sz.n + 1),
        out_specs=HBM,
        scratch_shapes=[
            pltpu.VMEM((pairs, cd, PAIR), BF16),
            pltpu.VMEM((region, TILE), BF16),
            pltpu.VMEM((2, ij, PAIR), BF16),
            pltpu.VMEM((ij, cd), BF16),
            pltpu.SemaphoreType.DMA((sz.n - 1,)),
            pltpu.SemaphoreType.DMA((2,)),
            pltpu.SemaphoreType.DMA((len(t2), 2)),
        ],
        input_output_aliases={2: 0},
        compiler_params=PARAMS,
        cost_estimate=COST,
        name="tail_part",
    )(info, late, begun, rest, *t2, *ends, *spread)


def last_hop(sz, length, info, place, late, t2, own, got, ends, lf, spread, begun):
    n = sz.n
    joined = pool(sz, length, info, lf, spread)
    came = [lax.ppermute(joined, "row", pair) for pair in ([(n - 2, n - 1)], [(1, 0)])]
    begun, rest = main_part(sz, 2, info, place, t2, own, got, ends, lf, begun)
    return tail_part(sz, info, late, t2, begun, rest, came, spread)


def tie(value, after):
    return lax.optimization_barrier((value, after))[0]


def body(n, n_col, t2_amps, v_ints, t2_mask, v_mask):
    sz = Sizes(n, *v_mask.shape)
    me = lax.axis_index("row")
    here = jnp.stack([me, lax.axis_index("col")])
    own, lf, screened = begin(sz, v_ints, t2_amps, v_mask, t2_mask)

    def hop(s, value, after=None):
        up, down = value
        if after is not None:
            up, down = tie(up, after), tie(down, after)
        pairs = [(i, i + 1) for i in range(s, n - 1)]
        back = [(n - 1 - i, n - 1 - j) for i, j in pairs]
        return lax.ppermute(up, "row", pairs), lax.ppermute(down, "row", back)

    def across(value, d):
        return lax.ppermute(value, "col", [(i, i ^ d) for i in range(n_col)])

    t2 = {0: screened}
    got = [hop(0, (own, own))]
    for d in range(2, n_col, 2):
        t2[d] = across(screened if d < 6 else tie(screened, t2[2]), d)
    for d in range(0, n_col, 2):
        t2[d + 1] = across(t2[d], 1)
    t2 = [t2[d] for d in range(n_col)]
    for s in range(1, n - 2):
        got.append(hop(s, got[-1], t2[2:5:2] if s == 1 else None))
    ends = [(n - 2, n - 1), (1, 0)]

    def last(c, after):
        return lax.ppermute(choose(sz, c, tie(here, after), *got[-1]), "row", ends)

    def leftovers(d, after):
        pairs = [(i, i ^ d) for i in range(n) if 0 < i ^ d < n - 1]
        return lax.ppermute(tie(lf, after), "row", pairs)

    spread = {1: leftovers(1, got[0])}
    first = last(0, (t2, spread[1]))
    need = longest(sz, here, own, got)
    need = lax.pmax(need, "col")
    second = last(1, need)
    spread.update({d: leftovers(d, need) for d in range(2, n)})
    spread = [spread[d] for d in range(1, n)]
    place, late, info = plan(sz, tie(here, need), own, got, first)
    told = lax.ppermute(tie(need, place), "row", ends)
    need = jnp.where(jnp.logical_or(me == 0, me == n - 1), told, need)[0]
    begun = main_part(sz, 1, info, place, t2, own, got, (first,))

    branch = sum((need > length).astype(jnp.int32) for length in sz.lengths[:-1])
    return lax.switch(
        branch,
        [functools.partial(last_hop, sz, length) for length in sz.lengths],
        info, place, late, t2, own, got, (first, second), lf, spread, begun,
    )


def solution(mesh):
    in_specs = (P("row", "col"), P("row", "col"), P("row", "col"), P("row", "col"))
    return jax.shard_map(
        functools.partial(body, mesh.shape["row"], mesh.shape["col"]),
        mesh=mesh,
        in_specs=in_specs,
        out_specs=P("row", "col"),
        check_vma=False,
    )
```

time: 249 us -> 163 us (0.65)
  waiting for transfers between devices: 205 us -> 55.7 us
  Pallas kernels: 0 us -> 53.4 us
  starting transfers between devices: 0.04 us -> 40.8 us
  matrix products: 23.7 us -> 0 us
  between operations: 13.4 us -> 1.68 us
  blocking collectives: 0 us -> 8.46 us
  other arithmetic: 5.48 us -> 0.07 us
    all_gather x2 -> x0, waiting for transfers between devices: 205 us -> none  [the longest x1 150 us: body(): lax.all_gather(masked_v, 'row', axis=0, tiled=True)]
    ppermute x0 -> x19, waiting for transfers between devices: none -> 55.7 us  [the longest x7 35.2 us: across(): return lax.ppermute(value, 'col', [(i, i ^ d) for i in range(n_col)])]
    pallas_call x0 -> x9, Pallas kernels: none -> 53.4 us  [the longest x2 30.8 us: main_part(): pl.pallas_call(functools.partial(main_kernel, sz, chunks, len(t2)), out_s...]
    ppermute x0 -> x19, starting transfers between devices: none -> 40.8 us  [the longest x3 17.2 us: leftovers(): return lax.ppermute(tie(lf, after), 'row', pairs)]
    dot_general x1 -> x0, matrix products: 23.7 us -> none  [body(): jnp.dot(amp_whole, lax.all_gather(masked_v, 'row', axis=0, tiled=True), p...]
    pmax x0 -> x1, blocking collectives: none -> 8.46 us  [body(): need = lax.pmax(need, 'col')]
    select_n x2 -> x0, other arithmetic: 4.7 us -> none  [the longest x1 3.45 us: body(): jnp.where(expand(v_mask, v_ints.shape[0], v_ints.shape[1]), v_ints, jnp.z...]
  transfers between devices with their start and end apart: 2 -> 19, of which waited for: 2 -> 5; matrix products, arithmetic and copies ran while one was open for 1% -> 0% of each run, Pallas kernels for 0% -> 25%
where the time goes in v1:
time: 163 us; the launch traced here: 162 us
  waiting for transfers between devices  55.7 us (34%)
  Pallas kernels  53.4 us (33%)
  starting transfers between devices  40.8 us (25%)
  blocking collectives  8.46 us (5%)
  between operations  1.68 us (1%)
    ppermute x7, waiting for transfers between devices, across(): return lax.ppermute(value, 'col', [(i, i ^ d) for i in range(n_col)])  35.2 us
    pallas_call x2, Pallas kernels, main_part(): pl.pallas_call(functools.partial(main_kernel, sz, chunks, len(t2)), out_s...  30.8 us
    ppermute x3, starting transfers between devices, leftovers(): return lax.ppermute(tie(lf, after), 'row', pairs)  17.2 us
    ppermute x3, waiting for transfers between devices, leftovers(): return lax.ppermute(tie(lf, after), 'row', pairs)  11.2 us
    ppermute x4, starting transfers between devices, hop(): return (lax.ppermute(up, 'row', pairs), lax.ppermute(down, 'row', back))  11.1 us
    ppermute x4, waiting for transfers between devices, hop(): return (lax.ppermute(up, 'row', pairs), lax.ppermute(down, 'row', back))  9.32 us
    pmax x1, blocking collectives, body(): need = lax.pmax(need, 'col')  8.46 us
    ppermute x7, starting transfers between devices, across(): return lax.ppermute(value, 'col', [(i, i ^ d) for i in range(n_col)])  6.57 us
  transfers between devices with their start and end apart: 19, of which 5 were waited for; matrix products, arithmetic and copies ran while one was open for 0% of the time, Pallas kernels for 25%

profile of v1, /device:TPU:0, one launch (start us, length us, event | category | flops | bytes accessed | tf_op | source)
XLA Modules:
  0.0 162.5 jit_solution(287558048051845967)
XLA Ops:
  0.0 4.2 %begin.1 = (bf16[6160,128]{1,0:T(8,128)(2,1)}, bf16[2048,128]{1,0:T(8,128)(2,1)}, bf16[2048,256]{1,0:T(8,128)(2,1)S(1)}) custom-call(s32[4,16]{1,0:T(4,128)} %v_mask_hbm.1, s32[4,16]{1,0:T(4,128)} %v_mask_hbm.1, s32[2,16]{1,0:T(2,128)} %bitcast.5, bf16[512,2048]{1,0:T(8,128)(2,1)} %v.1, bf16[2048,256]{1,0:T(8,128)(2,1)} %t2.1), custom_call_target="tpu_custom_call" | custom-call | tf_op jit(solution)/shard_map/begin/pallas_call | solution.py:92
  4.2 1.3 collective-permute-start.15
  5.5 6.7 %collective-permute-start.14 = (bf16[6160,128]{1,0:T(8,128)(2,1)}, bf16[6160,128]{1,0:T(8,128)(2,1)}, u32[]{:S(2)}, u32[]{:S(2)}) collective-permute-start(bf16[6160,128]{1,0:T(8,128)(2,1)} %get-tuple-element.524.refs_0_.refs_8_), channel_id=1, source_target_pairs={{0,8},{8,16},{16,24},{1,9},{9,17},{17,25},{2,10},{10,18},{18,26},{... | collective-permute-start | bytes 4730888 | tf_op jit(solution)/shard_map/ppermute | solution.py:521
  12.2 1.9 %collective-permute-start.16 = (bf16[2048,256]{1,0:T(8,128)(2,1)S(1)}, bf16[2048,256]{1,0:T(8,128)(2,1)S(1)}, u32[]{:S(2)}, u32[]{:S(2)}) collective-permute-start(bf16[2048,256]{1,0:T(8,128)(2,1)S(1)} %get-tuple-element.529.refs_0_), channel_id=1, source_target_pairs={{0,2},{1,3},{2,0},{3,1},{4,6},{5,7},{6,4},{7,5},{8,10},{9,11},{10,... | collective-permute-start | bytes 3145736 | tf_op jit(solution)/shard_map/ppermute | solution.py:524
  14.1 1.5 collective-permute-start.17
  15.6 21.2 %collective-permute-done.16.refs_2_ = bf16[2048,256]{1,0:T(8,128)(2,1)S(1)} collective-permute-done((bf16[2048,256]{1,0:T(8,128)(2,1)S(1)}, bf16[2048,256]{1,0:T(8,128)(2,1)S(1)}, u32[]{:S(2)}, u32[]{:S(2)}) %collective-permute-start.16) | collective-permute-done | bytes 1048608 | tf_op jit(solution)/shard_map/ppermute | solution.py:524
  36.8 2.6 %collective-permute-start.23 = (bf16[2048,256]{1,0:T(8,128)(2,1)S(1)}, bf16[2048,256]{1,0:T(8,128)(2,1)S(1)}, u32[]{:S(2)}, u32[]{:S(2)}) collective-permute-start(bf16[2048,256]{1,0:T(8,128)(2,1)S(1)} %get-tuple-element.529.refs_0_), channel_id=1, source_target_pairs={{0,6},{1,7},{2,4},{3,5},{4,2},{5,3},{6,0},{7,1},{8,14},{9,15},{10,... | collective-permute-start | bytes 3145736 | tf_op jit(solution)/shard_map/ppermute | solution.py:524
  39.4 4.5 %collective-permute-done.15.refs_2_.refs_10_ = bf16[6160,128]{1,0:T(8,128)(2,1)} collective-permute-done((bf16[6160,128]{1,0:T(8,128)(2,1)}, bf16[6160,128]{1,0:T(8,128)(2,1)}, u32[]{:S(2)}, u32[]{:S(2)}) %collective-permute-start.15) | collective-permute-done | bytes 1576992 | tf_op jit(solution)/shard_map/ppermute | solution.py:521
  43.9 1.3 collective-permute-start.19
  45.2 1.8 %collective-permute-start.18 = (bf16[6160,128]{1,0:T(8,128)(2,1)}, bf16[6160,128]{1,0:T(8,128)(2,1)}, u32[]{:S(2)}, u32[]{:S(2)}) collective-permute-start(bf16[6160,128]{1,0:T(8,128)(2,1)} %collective-permute-done.14.refs_1_.refs_9_), channel_id=1, source_target_pairs={{8,16},{16,24},{9,17},{17,25},{10,18},{18,26},{11,19},{19,27},{12,... | collective-permute-start | bytes 4730888 | tf_op jit(solution)/shard_map/ppermute | solution.py:521
  47.6 14.0 %collective-permute-done.23.refs_6_ = bf16[2048,256]{1,0:T(8,128)(2,1)S(1)} collective-permute-done((bf16[2048,256]{1,0:T(8,128)(2,1)S(1)}, bf16[2048,256]{1,0:T(8,128)(2,1)S(1)}, u32[]{:S(2)}, u32[]{:S(2)}) %collective-permute-start.23) | collective-permute-done | bytes 1048608 | tf_op jit(solution)/shard_map/ppermute | solution.py:524
  61.6 1.0 copy-done.8
  62.6 3.1 %collective-permute-start.25 = (bf16[2048,128]{1,0:T(8,128)(2,1)}, bf16[2048,128]{1,0:T(8,128)(2,1)}, u32[]{:S(2)}, u32[]{:S(2)}) collective-permute-start(bf16[2048,128]{1,0:T(8,128)(2,1)} %get-tuple-element.536), channel_id=1, source_target_pairs={{0,8},{24,16},{1,9},{25,17},{2,10},{26,18},{3,11},{27,19},{4,12},{... | collective-permute-start | bytes 1572872 | tf_op jit(solution)/shard_map/ppermute | solution.py:542
  65.7 11.2 %collective-permute-done.25 = bf16[2048,128]{1,0:T(8,128)(2,1)} collective-permute-done((bf16[2048,128]{1,0:T(8,128)(2,1)}, bf16[2048,128]{1,0:T(8,128)(2,1)}, u32[]{:S(2)}, u32[]{:S(2)}) %collective-permute-start.25) | collective-permute-done | bytes 524320 | tf_op jit(solution)/shard_map/ppermute | solution.py:542
  76.9 4.8 %collective-permute-done.19.refs_4_.down.refs_12_ = bf16[6160,128]{1,0:T(8,128)(2,1)} collective-permute-done((bf16[6160,128]{1,0:T(8,128)(2,1)}, bf16[6160,128]{1,0:T(8,128)(2,1)}, u32[]{:S(2)}, u32[]{:S(2)}) %collective-permute-start.19) | collective-permute-done | bytes 1576992 | tf_op jit(solution)/shard_map/ppermute | solution.py:521
  81.8 1.7 %choose.2 = bf16[3600,128]{1,0:T(8,128)(2,1)S(1)} custom-call(s32[2]{0:T(128)S(1)} %pad_add_fusion.here, bf16[6160,128]{1,0:T(8,128)(2,1)} %collective-permute-done.18.refs_3_.up.refs_11_, bf16[6160,128]{1,0:T(8,128)(2,1)} %collective-permute-done.19.refs_4_.down.refs_12_), custom_call_target="tpu_custom_call" | custom-call | tf_op jit(solution)/shard_map/choose/pallas_call | solution.py:245
  83.5 1.3 collective-permute-start.26
  84.8 2.1 %longest.1 = s32[1]{0:T(128)} custom-call(s32[2]{0:T(128)} %copy-done, bf16[6160,128]{1,0:T(8,128)(2,1)} %get-tuple-element.524.refs_0_.refs_8_, bf16[6160,128]{1,0:T(8,128)(2,1)} %collective-permute-done.14.refs_1_.refs_9_, bf16[6160,128]{1,0:T(8,128)(2,1)} %collective-permute-done.15.refs_2_.refs_10_, ...), custom_call_target="tpu_custom_call" | custom-call | tf_op jit(solution)/shard_map/longest/pallas_call | solution.py:142
  86.9 8.5 %pmax.7 = s32[1]{0:T(128)} all-reduce(s32[1]{0:T(128)} %longest.1), channel_id=1, replica_groups=mesh['row'=4,'col'=8] {'col'}, use_global_device_ids=true, to_apply=%region_0.0 | all-reduce | flops 1 | bytes 8 | tf_op jit(solution)/shard_map/pmax | solution.py:547
  96.0 1.6 %choose.3 = bf16[2560,128]{1,0:T(8,128)(2,1)S(1)} custom-call(s32[2]{0:T(128)S(1)} %copy-done.1, bf16[6160,128]{1,0:T(8,128)(2,1)} %collective-permute-done.18.refs_3_.up.refs_11_, bf16[6160,128]{1,0:T(8,128)(2,1)} %collective-permute-done.19.refs_4_.down.refs_12_), custom_call_target="tpu_custom_call" | custom-call | tf_op jit(solution)/shard_map/choose/pallas_call | solution.py:245
  97.6 1.3 collective-permute-start.28
  98.9 0.7 collective-permute-start.30
  99.6 13.5 %collective-permute-start.29 = (bf16[2048,128]{1,0:T(8,128)(2,1)}, bf16[2048,128]{1,0:T(8,128)(2,1)}, u32[]{:S(2)}, u32[]{:S(2)}) collective-permute-start(bf16[2048,128]{1,0:T(8,128)(2,1)} %get-tuple-element.536), channel_id=1, source_target_pairs={{0,16},{24,8},{1,17},{25,9},{2,18},{26,10},{3,19},{27,11},{4,20},{... | collective-permute-start | bytes 1572872 | tf_op jit(solution)/shard_map/ppermute | solution.py:542
  113.1 5.4 %plan.1 = (s32[256]{0:T(256)S(1)}, s32[256]{0:T(256)S(1)}, s32[10]{0:T(128)S(1)}) custom-call(s32[2]{0:T(128)} %copy-done, bf16[6160,128]{1,0:T(8,128)(2,1)} %get-tuple-element.524.refs_0_.refs_8_, bf16[6160,128]{1,0:T(8,128)(2,1)} %collective-permute-done.14.refs_1_.refs_9_, bf16[6160,128]{1,0:T(8,128)(2,1)} %collective-permute-done.15.refs_2_.refs_10_, ...), custom_call_target="tpu_custom_call" | custom-call | tf_op jit(solution)/shard_map/plan/pallas_call | solution.py:213
  118.6 1.3 collective-permute-start.27
  119.9 16.6 %main_part.15 = bf16[2048,2048]{1,0:T(8,128)(2,1)} custom-call(s32[10]{0:T(128)S(1)} %get-tuple-element.535.info, s32[256]{0:T(256)S(1)} %get-tuple-element.533.place, bf16[2048,256]{1,0:T(8,128)(2,1)S(1)} %get-tuple-element.529.refs_0_, bf16[2048,256]{1,0:T(8,128)(2,1)} %collective-permute-done.20.refs_1_, bf16[2048,256]{1,0:T(8,128)(2,1)S(1)} %copy-done.3, ...), custom_call_target="tpu_custom_call" | custom-call | flops 1048576 | bytes 4096 | tf_op jit(solution)/shard_map/main_part/pallas_call | solution.py:397
  137.8 24.4 %conditional.1 = (bf16[2048,2048]{1,0:T(8,128)(2,1)}) conditional(s32[]{:T(128)} %bitcast.4, (s32[10]{0:T(128)S(1)}, s32[256]{0:T(256)S(1)}, bf16[2048,256]{1,0:T(8,128)(2,1)S(1)}, bf16[2048,256]{1,0:T(8,128)(2,1)}, bf16[2048,256]{1,0:T(8,128)(2,1)S(1)}, /*index=5*/bf16[2048,256]{1,0:T(8,128)(2,1)}, ...), branch_computations={%region_1.2_spmd, %region_2.3_spmd, %region_3.4_spmd, %region_4.5_... | conditional | flops 2097152 | bytes 12591192 | solution.py:557
  138.1 1.4 pool.9
  139.4 1.3 collective-permute-start.5
  140.7 0.7 collective-permute-start.4
  141.4 14.1 %main_part.10 = (bf16[2048,2048]{1,0:T(8,128)(2,1)}, bf16[2,2048,256]{2,1,0:T(8,128)(2,1)S(1)}) custom-call(s32[10]{0:T(128)S(1)} %get-tuple-element.385.info, s32[256]{0:T(256)S(1)} %get-tuple-element.387.place, bf16[2048,256]{1,0:T(8,128)(2,1)S(1)} %get-tuple-element.388.refs_0_, ...), custom_call_target="tpu_custom_call", output_to_operand_aliasing={{0}: (18, {})} | custom-call | flops 1048576 | bytes 4096 | tf_op jit(solution)/shard_map/cond/branch_2_fun/main_part/pallas_call | solution.py:397
  155.6 6.1 %tail_part.9 = bf16[2048,2048]{1,0:T(8,128)(2,1)} custom-call(s32[10]{0:T(128)S(1)} %get-tuple-element.385.info, s32[256]{0:T(256)S(1)} %get-tuple-element.386.late, bf16[2048,2048]{1,0:T(8,128)(2,1)} %get-tuple-element.405.begun, bf16[2,2048,256]{2,1,0:T(8,128)(2,1)S(1)} %get-tuple-element.406.rest, ...), custom_call_target="tpu_custom_call", output_to_operand_aliasing={{}: (2, {})} | custom-call | flops 1048576 | bytes 4096 | tf_op jit(solution)/shard_map/cond/branch_2_fun/tail_part/pallas_call | solution.py:476
  (38 shorter events, 1.3 us)
Async XLA Ops:
  4.2 39.7 %collective-permute-start.15 = (bf16[6160,128]{1,0:T(8,128)(2,1)}, bf16[6160,128]{1,0:T(8,128)(2,1)}, u32[]{:S(2)}, u32[]{:S(2)}) collective-permute-start(bf16[6160,128]{1,0:T(8,128)(2,1)} %get-tuple-element.524.refs_0_.refs_8_), channel_id=1, source_target_pairs={{24,16},{16,8},{8,0},{25,17},{17,9},{9,1},{26,18},{18,10},{10,2},{... | collective-permute-start | bytes 4730888 | tf_op jit(solution)/shard_map/ppermute | solution.py:521
  5.5 39.7 %collective-permute-start.14 = (bf16[6160,128]{1,0:T(8,128)(2,1)}, bf16[6160,128]{1,0:T(8,128)(2,1)}, u32[]{:S(2)}, u32[]{:S(2)}) collective-permute-start(bf16[6160,128]{1,0:T(8,128)(2,1)} %get-tuple-element.524.refs_0_.refs_8_), channel_id=1, source_target_pairs={{0,8},{8,16},{16,24},{1,9},{9,17},{17,25},{2,10},{10,18},{18,26},{... | collective-permute-start | bytes 4730888 | tf_op jit(solution)/shard_map/ppermute | solution.py:521
  12.2 24.6 %collective-permute-start.16 = (bf16[2048,256]{1,0:T(8,128)(2,1)S(1)}, bf16[2048,256]{1,0:T(8,128)(2,1)S(1)}, u32[]{:S(2)}, u32[]{:S(2)}) collective-permute-start(bf16[2048,256]{1,0:T(8,128)(2,1)S(1)} %get-tuple-element.529.refs_0_), channel_id=1, source_target_pairs={{0,2},{1,3},{2,0},{3,1},{4,6},{5,7},{6,4},{7,5},{8,10},{9,11},{10,... | collective-permute-start | bytes 3145736 | tf_op jit(solution)/shard_map/ppermute | solution.py:524
  14.1 25.3 %collective-permute-start.17 = (bf16[2048,256]{1,0:T(8,128)(2,1)S(1)}, bf16[2048,256]{1,0:T(8,128)(2,1)S(1)}, u32[]{:S(2)}, u32[]{:S(2)}) collective-permute-start(bf16[2048,256]{1,0:T(8,128)(2,1)S(1)} %get-tuple-element.529.refs_0_), channel_id=1, source_target_pairs={{0,4},{1,5},{2,6},{3,7},{4,0},{5,1},{6,2},{7,3},{8,12},{9,13},{10,... | collective-permute-start | bytes 3145736 | tf_op jit(solution)/shard_map/ppermute | solution.py:524
  15.6 31.4 %collective-permute-start.20 = (bf16[2048,256]{1,0:T(8,128)(2,1)S(1)}, bf16[2048,256]{1,0:T(8,128)(2,1)}, u32[]{:S(2)}, u32[]{:S(2)}) collective-permute-start(bf16[2048,256]{1,0:T(8,128)(2,1)S(1)} %get-tuple-element.529.refs_0_), channel_id=1, source_target_pairs={{0,1},{1,0},{2,3},{3,2},{4,5},{5,4},{6,7},{7,6},{8,9},{9,8},{10,11... | collective-permute-start | bytes 3145736 | tf_op jit(solution)/shard_map/ppermute | solution.py:524
  36.8 45.0 %copy-start.2 = (bf16[2048,256]{1,0:T(8,128)(2,1)}, bf16[2048,256]{1,0:T(8,128)(2,1)S(1)}, u32[]{:S(2)}) copy-start(bf16[2048,256]{1,0:T(8,128)(2,1)S(1)} %collective-permute-done.16.refs_2_) | copy-start | bytes 3145732
  36.8 24.7 %collective-permute-start.23 = (bf16[2048,256]{1,0:T(8,128)(2,1)S(1)}, bf16[2048,256]{1,0:T(8,128)(2,1)S(1)}, u32[]{:S(2)}, u32[]{:S(2)}) collective-permute-start(bf16[2048,256]{1,0:T(8,128)(2,1)S(1)} %get-tuple-element.529.refs_0_), channel_id=1, source_target_pairs={{0,6},{1,7},{2,4},{3,5},{4,2},{5,3},{6,0},{7,1},{8,14},{9,15},{10,... | collective-permute-start | bytes 3145736 | tf_op jit(solution)/shard_map/ppermute | solution.py:524
  39.4 22.1 %copy-start.4 = (bf16[2048,256]{1,0:T(8,128)(2,1)}, bf16[2048,256]{1,0:T(8,128)(2,1)S(1)}, u32[]{:S(2)}) copy-start(bf16[2048,256]{1,0:T(8,128)(2,1)S(1)} %collective-permute-done.17.refs_4_) | copy-start | bytes 3145732
  43.9 37.9 %collective-permute-start.19 = (bf16[6160,128]{1,0:T(8,128)(2,1)}, bf16[6160,128]{1,0:T(8,128)(2,1)}, u32[]{:S(2)}, u32[]{:S(2)}) collective-permute-start(bf16[6160,128]{1,0:T(8,128)(2,1)} %collective-permute-done.15.refs_2_.refs_10_), channel_id=1, source_target_pairs={{16,8},{8,0},{17,9},{9,1},{18,10},{10,2},{19,11},{11,3},{20,12},{1... | collective-permute-start | bytes 4730888 | tf_op jit(solution)/shard_map/ppermute | solution.py:521
  45.2 36.6 %collective-permute-start.18 = (bf16[6160,128]{1,0:T(8,128)(2,1)}, bf16[6160,128]{1,0:T(8,128)(2,1)}, u32[]{:S(2)}, u32[]{:S(2)}) collective-permute-start(bf16[6160,128]{1,0:T(8,128)(2,1)} %collective-permute-done.14.refs_1_.refs_9_), channel_id=1, source_target_pairs={{8,16},{16,24},{9,17},{17,25},{10,18},{18,26},{11,19},{19,27},{12,... | collective-permute-start | bytes 4730888 | tf_op jit(solution)/shard_map/ppermute | solution.py:521
  47.0 14.5 %collective-permute-start.22 = (bf16[2048,256]{1,0:T(8,128)(2,1)S(1)}, bf16[2048,256]{1,0:T(8,128)(2,1)S(1)}, u32[]{:S(2)}, u32[]{:S(2)}) collective-permute-start(bf16[2048,256]{1,0:T(8,128)(2,1)S(1)} %collective-permute-done.17.refs_4_), channel_id=1, source_target_pairs={{0,1},{1,0},{2,3},{3,2},{4,5},{5,4},{6,7},{7,6},{8,9},{9,8},{10,11... | collective-permute-start | bytes 3145736 | tf_op jit(solution)/shard_map/ppermute | solution.py:524
  47.0 18.7 %collective-permute-start.21 = (bf16[2048,256]{1,0:T(8,128)(2,1)S(1)}, bf16[2048,256]{1,0:T(8,128)(2,1)}, u32[]{:S(2)}, u32[]{:S(2)}) collective-permute-start(bf16[2048,256]{1,0:T(8,128)(2,1)S(1)} %collective-permute-done.16.refs_2_), channel_id=1, source_target_pairs={{0,1},{1,0},{2,3},{3,2},{4,5},{5,4},{6,7},{7,6},{8,9},{9,8},{10,11... | collective-permute-start | bytes 3145736 | tf_op jit(solution)/shard_map/ppermute | solution.py:524
  61.5 25.4 %copy-start.6 = (bf16[2048,256]{1,0:T(8,128)(2,1)}, bf16[2048,256]{1,0:T(8,128)(2,1)S(1)}, u32[]{:S(2)}) copy-start(bf16[2048,256]{1,0:T(8,128)(2,1)S(1)} %collective-permute-done.23.refs_6_) | copy-start | bytes 3145732
  61.5 15.4 %collective-permute-start.24 = (bf16[2048,256]{1,0:T(8,128)(2,1)S(1)}, bf16[2048,256]{1,0:T(8,128)(2,1)}, u32[]{:S(2)}, u32[]{:S(2)}) collective-permute-start(bf16[2048,256]{1,0:T(8,128)(2,1)S(1)} %collective-permute-done.23.refs_6_), channel_id=1, source_target_pairs={{0,1},{1,0},{2,3},{3,2},{4,5},{5,4},{6,7},{7,6},{8,9},{9,8},{10,11... | collective-permute-start | bytes 3145736 | tf_op jit(solution)/shard_map/ppermute | solution.py:524
  61.6 1.0 copy-start.8
  62.6 14.4 %collective-permute-start.25 = (bf16[2048,128]{1,0:T(8,128)(2,1)}, bf16[2048,128]{1,0:T(8,128)(2,1)}, u32[]{:S(2)}, u32[]{:S(2)}) collective-permute-start(bf16[2048,128]{1,0:T(8,128)(2,1)} %get-tuple-element.536), channel_id=1, source_target_pairs={{0,8},{24,16},{1,9},{25,17},{2,10},{26,18},{3,11},{27,19},{4,12},{... | collective-permute-start | bytes 1572872 | tf_op jit(solution)/shard_map/ppermute | solution.py:542
  65.7 19.1 %copy-start = (s32[2]{0:T(128)}, s32[2]{0:T(128)S(1)}, u32[]{:S(2)}) copy-start(s32[2]{0:T(128)S(1)} %pad_add_fusion.here) | copy-start | bytes 28
  83.5 29.6 %collective-permute-start.26 = (bf16[3600,128]{1,0:T(8,128)(2,1)S(1)}, bf16[3600,128]{1,0:T(8,128)(2,1)}, u32[]{:S(2)}, u32[]{:S(2)}) collective-permute-start(bf16[3600,128]{1,0:T(8,128)(2,1)S(1)} %choose.2), channel_id=1, source_target_pairs={{16,24},{8,0},{17,25},{9,1},{18,26},{10,2},{19,27},{11,3},{20,28},... | collective-permute-start | bytes 2764808 | tf_op jit(solution)/shard_map/ppermute | solution.py:538
  95.4 0.6 copy-start.1
  97.6 38.9 %collective-permute-start.28 = (bf16[2560,128]{1,0:T(8,128)(2,1)S(1)}, bf16[2560,128]{1,0:T(8,128)(2,1)}, u32[]{:S(2)}, u32[]{:S(2)}) collective-permute-start(bf16[2560,128]{1,0:T(8,128)(2,1)S(1)} %choose.3), channel_id=1, source_target_pairs={{16,24},{8,0},{17,25},{9,1},{18,26},{10,2},{19,27},{11,3},{20,28},... | collective-permute-start | bytes 1966088 | tf_op jit(solution)/shard_map/ppermute | solution.py:538
  98.9 37.6 %collective-permute-start.30 = (bf16[2048,128]{1,0:T(8,128)(2,1)}, bf16[2048,128]{1,0:T(8,128)(2,1)S(1)}, u32[]{:S(2)}, u32[]{:S(2)}) collective-permute-start(bf16[2048,128]{1,0:T(8,128)(2,1)} %get-tuple-element.536), channel_id=1, source_target_pairs={{8,16},{16,8},{9,17},{17,9},{10,18},{18,10},{11,19},{19,11},{12,20... | collective-permute-start | bytes 1572872 | tf_op jit(solution)/shard_map/ppermute | solution.py:542
  99.6 36.9 %collective-permute-start.29 = (bf16[2048,128]{1,0:T(8,128)(2,1)}, bf16[2048,128]{1,0:T(8,128)(2,1)}, u32[]{:S(2)}, u32[]{:S(2)}) collective-permute-start(bf16[2048,128]{1,0:T(8,128)(2,1)} %get-tuple-element.536), channel_id=1, source_target_pairs={{0,16},{24,8},{1,17},{25,9},{2,18},{26,10},{3,19},{27,11},{4,20},{... | collective-permute-start | bytes 1572872 | tf_op jit(solution)/shard_map/ppermute | solution.py:542
  113.1 6.8 %copy-start.3 = (bf16[2048,256]{1,0:T(8,128)(2,1)S(1)}, bf16[2048,256]{1,0:T(8,128)(2,1)}, u32[]{:S(2)}) copy-start(bf16[2048,256]{1,0:T(8,128)(2,1)} %copy-done.2) | copy-start | bytes 3145732
  118.6 18.0 %collective-permute-start.27 = (s32[1]{0:T(128)}, s32[1]{0:T(128)}, u32[]{:S(2)}, u32[]{:S(2)}) collective-permute-start(s32[1]{0:T(128)} %pmax.7), channel_id=1, source_target_pairs={{16,24},{8,0},{17,25},{9,1},{18,26},{10,2},{19,27},{11,3},{20,28},... | collective-permute-start | bytes 20 | tf_op jit(solution)/shard_map/ppermute | solution.py:552
  119.9 17.9 %copy-start.5 = (bf16[2048,256]{1,0:T(8,128)(2,1)S(1)}, bf16[2048,256]{1,0:T(8,128)(2,1)}, u32[]{:S(2)}) copy-start(bf16[2048,256]{1,0:T(8,128)(2,1)} %copy-done.4) | copy-start | bytes 3145732
  119.9 17.9 %copy-start.7 = (bf16[2048,256]{1,0:T(8,128)(2,1)S(1)}, bf16[2048,256]{1,0:T(8,128)(2,1)}, u32[]{:S(2)}) copy-start(bf16[2048,256]{1,0:T(8,128)(2,1)} %copy-done.6) | copy-start | bytes 3145732
  119.9 17.9 %copy-start.9 = (bf16[2048,256]{1,0:T(8,128)(2,1)S(1)}, bf16[2048,256]{1,0:T(8,128)(2,1)}, u32[]{:S(2)}) copy-start(bf16[2048,256]{1,0:T(8,128)(2,1)} %copy-done.8) | copy-start | bytes 3145732
  139.4 16.1 %collective-permute-start.5 = (bf16[1536,128]{1,0:T(8,128)(2,1)S(1)}, bf16[1536,128]{1,0:T(8,128)(2,1)S(1)}, u32[]{:S(2)}, u32[]{:S(2)}) collective-permute-start(bf16[1536,128]{1,0:T(8,128)(2,1)S(1)} %pool.9), channel_id=1, source_target_pairs={{8,0},{9,1},{10,2},{11,3},{12,4},{13,5},{14,6},{15,7}} | collective-permute-start | bytes 1179656 | tf_op jit(solution)/shard_map/cond/branch_2_fun/ppermute | solution.py:500
  140.7 14.8 %collective-permute-start.4 = (bf16[1536,128]{1,0:T(8,128)(2,1)S(1)}, bf16[1536,128]{1,0:T(8,128)(2,1)S(1)}, u32[]{:S(2)}, u32[]{:S(2)}) collective-permute-start(bf16[1536,128]{1,0:T(8,128)(2,1)S(1)} %pool.9), channel_id=1, source_target_pairs={{16,24},{17,25},{18,26},{19,27},{20,28},{21,29},{22,30},{23,31}} | collective-permute-start | bytes 1179656 | tf_op jit(solution)/shard_map/cond/branch_2_fun/ppermute | solution.py:500

commit v2 on v1

--- a/solution.py
+++ b/solution.py
@@ -16,7 +16,7 @@
 VMEM = pl.BlockSpec(memory_space=pltpu.VMEM)
 ANY = pl.BlockSpec(memory_space=pl.ANY)
 HBM = pl.BlockSpec(memory_space=pltpu.HBM)
-PARAMS = pltpu.CompilerParams(vmem_limit_bytes=48 << 20)
+PARAMS = pltpu.CompilerParams(vmem_limit_bytes=40 << 20)
 COST = pl.CostEstimate(flops=1 << 20, bytes_accessed=1 << 12, transcendentals=0)
 LENGTHS = (8, 10, 12, 14, 16, 20)
 FIRST = 28
@@ -39,6 +39,7 @@
         self.left = self.all - self.main
         self.stream = (n - 1) * self.left
         self.pairs = n_tiles // 2
+        self.near = n // 2
         self.sure = (self.main // k_tiles) // 2
         lengths = {-(-f * self.stream // 48) for f in LENGTHS}
         self.lengths = sorted(lengths | {self.stream})
@@ -152,13 +153,62 @@
     )(here, *ops)
 
 
-def from_source(sz, me, own, got, act):
+def from_source(sz, me, own, got, act, take=None):
     for m in range(sz.n):
 
         @pl.when(me == m)
         def _():
             for z in range(sz.n):
-                act(z, own if z == m else got[abs(z - m) - 1][0 if z < m else 1])
+                if take is None or take(m, z):
+                    act(z, own if z == m else got[abs(z - m) - 1][0 if z < m else 1])
+
+
+def near_plan_kernel(sz, here, own, *refs):
+    h = sz.near
+    parts, (place, notes, wide, masks, note_sem, mask_sem) = refs[: 2 * h - 2], refs[2 * h - 2 :]
+
+    def note_copy(z, ref):
+        at = ref.at[pl.ds(0, NOTE), :]
+        return pltpu.make_async_copy(at, notes.at[pl.ds(z % h * NOTE, NOTE), :], note_sem.at[z % h])
+
+    got = [parts[2 * s : 2 * s + 2] for s in range(h - 1)]
+    from_source(sz, here[0], own, got, lambda z, ref: note_copy(z, ref).start(), lambda m, z: m // h == z // h)
+    for z in range(h):
+        note_copy(z, own).wait()
+    wide[...] = notes[...].astype(jnp.int32)
+    mask_copy = pltpu.make_async_copy(wide, masks, mask_sem)
+    mask_copy.start()
+    mask_copy.wait()
+
+    def column(c, counts):
+        counts = list(counts)
+        for z in range(h):
+            for k in range(sz.kd):
+                kept, p = masks[z * NOTE + k, c] > 0, counts[z]
+                at = jnp.where(jnp.logical_and(kept, p < sz.main), z * sz.main + p, h * sz.main)
+                place[(c * h + z) * sz.kd + k] = at
+                counts[z] = p + kept.astype(jnp.int32)
+        return tuple(counts)
+
+    lax.fori_loop(0, 2 * sz.sure, column, (jnp.int32(0),) * h)
+
+
+def near_plan(sz, here, own, got):
+    h, ops = sz.near, (own, *(part for hop in got for part in hop))
+    return pl.pallas_call(
+        functools.partial(near_plan_kernel, sz),
+        out_shape=jax.ShapeDtypeStruct((2 * sz.sure * h * sz.kd,), jnp.int32),
+        in_specs=[SMEM] + [ANY] * len(ops),
+        out_specs=SMEM,
+        scratch_shapes=[
+            pltpu.VMEM((h * NOTE, TILE), BF16),
+            pltpu.VMEM((h * NOTE, TILE), jnp.int32),
+            pltpu.SMEM((h * NOTE, TILE), jnp.int32),
+            pltpu.SemaphoreType.DMA((h,)),
+            pltpu.SemaphoreType.DMA,
+        ],
+        name="near_plan",
+    )(here, *ops)
 
 
 def plan_kernel(sz, here, *refs):
@@ -188,11 +238,9 @@
                 kept, p = masks[z * NOTE + k, c] > 0, counts[z]
                 place[i] = jnp.where(jnp.logical_and(kept, p < have), z * sz.all + p, n * sz.all)
                 late[i] = jnp.where(jnp.logical_and(kept, p >= have), p - sz.main, -1)
-                over = jnp.logical_and(kept, p >= sz.first)
-                firsts[z] = jnp.where(over, jnp.minimum(firsts[z], c), firsts[z])
-                over = jnp.logical_and(kept, p >= have)
-                seconds[z] = jnp.where(over, jnp.minimum(seconds[z], c), seconds[z])
                 counts[z] = p + kept.astype(jnp.int32)
+            firsts[z] = jnp.minimum(firsts[z], jnp.where(counts[z] > sz.first, c, sz.nd))
+            seconds[z] = jnp.minimum(seconds[z], jnp.where(counts[z] > have, c, sz.nd))
         return tuple(counts + firsts + seconds)
 
     start = (jnp.int32(0),) * n + (jnp.int32(sz.nd),) * (2 * n)
@@ -200,7 +248,7 @@
     lefts = [jnp.maximum(c - sz.main, 0) for c in out[:n]]
     info[0] = me
     info[1] = jnp.int32(0)
-    info[2] = functools.reduce(jnp.minimum, out[n : 2 * n], jnp.int32(sz.nd - 2)) // 2
+    info[2] = functools.reduce(jnp.minimum, out[n : 2 * n], jnp.int32(2 * sz.sure)) // 2
     info[3] = functools.reduce(jnp.minimum, out[2 * n :], jnp.int32(sz.nd - 2)) // 2
     info[4] = jnp.int32(sz.pairs)
     info[5] = here[1]
@@ -230,27 +278,30 @@
     )(here, *ops)
 
 
-def choose_kernel(sz, c, here, up, down, out, sem):
+def choose_kernel(sz, c, here, need, up, down, out, sem):
     at = sz.cut(c)[2]
+    size = out.shape[0] - at.size
+    if size:
+        out[:size, :] = jnp.full((size, TILE), need[0].astype(jnp.float32)).astype(BF16)
     for mine, x in ((here[0] == sz.n - 2, up), (here[0] != sz.n - 2, down)):
 
         @pl.when(mine)
         def _():
-            copy = pltpu.make_async_copy(x.at[at, :], out, sem)
+            copy = pltpu.make_async_copy(x.at[at, :], out.at[pl.ds(size, at.size), :], sem)
             copy.start()
             copy.wait()
 
 
-def choose(sz, c, here, up, down):
+def choose(sz, c, here, need, up, down):
     return pl.pallas_call(
         functools.partial(choose_kernel, sz, c),
-        out_shape=jax.ShapeDtypeStruct((sz.cut(c)[2].size, TILE), BF16),
-        in_specs=[SMEM, ANY, ANY],
+        out_shape=jax.ShapeDtypeStruct((sz.cut(c)[2].size + c * NOTE, TILE), BF16),
+        in_specs=[SMEM, SMEM, ANY, ANY],
         out_specs=VMEM,
         scratch_shapes=[pltpu.SemaphoreType.DMA],
         compiler_params=PARAMS,
         name="choose",
-    )(here, up, down)
+    )(here, need, up, down)
 
 
 def pool_kernel(sz, length, info, lf, *refs):
@@ -281,32 +332,62 @@
 
 
 def out_copy(out, held, sem, slot, pair):
+    if len(out.shape) == 3:
+        return pltpu.make_async_copy(held.at[slot], out.at[pair], sem.at[slot])
     return pltpu.make_async_copy(
         held.at[slot], out.at[:, pl.ds(pl.multiple_of(pair * PAIR, PAIR), PAIR)], sem.at[slot]
     )
 
 
-def t2_copies(info, t2, t2_v, sem, r):
-    half, wide = t2_v.shape[0] // 2, t2_v.shape[1] // len(t2)
-    at = pl.ds(pl.multiple_of(r * half, half), half)
-    for d, block in enumerate(t2):
-        to = t2_v.at[at, pl.ds(pl.multiple_of((info[5] ^ d) * wide, wide), wide)]
-        yield pltpu.make_async_copy(block.at[at, :], to, sem.at[d, r])
-
-
-def multiply(lo, hi, build, info, t2, t2_v, t2_sem, out, held, sem):
+def t2_copies(act, col, part, t2, t2_v, sem, rs=(0, 1)):
+    half, wide, nh = t2_v.shape[0] // 2, t2_v.shape[1] // len(t2), len(t2) // 2
+    mine = col // nh == part
+    for which, ds in ((mine, range(nh)), (jnp.logical_not(mine), range(nh, 2 * nh))):
+
+        @pl.when(which)
+        def _():
+            for r in rs:
+                at = pl.ds(pl.multiple_of(r * half, half), half)
+                for d in ds:
+                    to = t2_v.at[at, pl.ds(pl.multiple_of((col ^ d) * wide, wide), wide)]
+                    act(pltpu.make_async_copy(t2[d].at[at, :], to, sem.at[d, r]))
+
+
+def start(copy):
+    copy.start()
+
+
+def wait(copy):
+    copy.wait()
+
+
+def multiply(lo, hi, build, t2_wait, t2_v, out, held, sem, span=slice(None), acc=None, acc_v=None, acc_sem=None):
     half = held.shape[1] // 2
+
+    def acc_copy(pair, slot):
+        return pltpu.make_async_copy(acc.at[pair], acc_v.at[slot], acc_sem.at[slot])
+
+    if acc is not None:
+
+        @pl.when(lo < hi)
+        def _():
+            acc_copy(lo, 0).start()
 
     @pl.when(lo >= hi)
     def _():
-        for r in range(2):
-            for copy in t2_copies(info, t2, t2_v, t2_sem, r):
-                copy.wait()
+        t2_wait((0, 1))
 
     @pl.loop(lo, hi)
     def _(pair):
         slot = lax.rem(pair - lo, 2)
         b = build(pair)
+        if acc is not None:
+
+            @pl.when(pair + 1 < hi)
+            def _():
+                acc_copy(pair + 1, 1 - slot).start()
+
+            acc_copy(pair, slot).wait()
 
         @pl.when(pair >= lo + 2)
         def _():
@@ -316,13 +397,13 @@
         def _(r):
             @pl.when(pair == lo)
             def _():
-                for copy in t2_copies(info, t2, t2_v, t2_sem, r):
-                    copy.wait()
+                t2_wait((r,))
 
             at = pl.ds(pl.multiple_of(r * half, half), half)
-            held[slot, at, :] = jnp.dot(
-                t2_v[at, :], b[...], preferred_element_type=jnp.float32
-            ).astype(BF16)
+            product = jnp.dot(t2_v[at, span], b[...], preferred_element_type=jnp.float32)
+            if acc is not None:
+                product = product + acc_v[slot, at, :]
+            held[slot, at, :] = product.astype(held.dtype)
 
         out_copy(out, held, sem, slot, pair).start()
 
@@ -340,71 +421,156 @@
     got, refs = [refs[2 * s : 2 * s + 2] for s in range(n - 2)], refs[2 * (n - 2) :]
     ends, refs = refs[:chunks], refs[chunks:]
     if chunks == 2:
-        lf, begun, out, rest, packed, b, held, t2_v, in_sem, out_sem, t2_sem = refs
+        lf, acc, begun, out, rest, t2_v, packed, b, held, acc_v, in_sem, out_sem, acc_sem, t2_sem = refs
     else:
-        out, packed, b, held, t2_v, in_sem, out_sem, t2_sem = refs
-    me = info[0]
+        acc, out, packed, b, held, acc_v, t2_v, in_sem, out_sem, acc_sem, t2_sem = refs
+    me, col, h = info[0], info[5], sz.near
+    far = jnp.where(me < h, h, 0)
 
     def chunk_copy(ref, z, c):
         start, count, at = sz.cut(c)
         size = count * TILE
-        first = at.start + at.size - size if ref.shape[0] > at.size else ref.shape[0] - size
+        first = at.start + at.size - size if ref.shape[0] == NOTE + sz.main * TILE else ref.shape[0] - size
         to = packed.at[pl.ds((z * sz.all + start) * TILE, size), :]
         return pltpu.make_async_copy(ref.at[pl.ds(first, size), :], to, in_sem.at[z, c])
 
-    for c in range(chunks):
-        parts = got + [(ends[c], ends[c])]
-        from_source(sz, me, own, parts, lambda z, ref: chunk_copy(ref, z, c).start())
+    def start_chunks(take):
+        for c in range(chunks):
+            parts = got + [(ends[c], ends[c])]
+            from_source(sz, me, own, parts, lambda z, ref: chunk_copy(ref, z, c).start(), take)
+
+    def wait_chunks(first):
+        for i in range(h):
+            for c in range(chunks):
+                chunk_copy(own, first + i, c).wait()
+
+    def t2_part(act, part, rs):
+        t2_copies(act, col, part, t2, t2_v, t2_sem, rs)
+
+    far_part = far // h
+    start_chunks(lambda m, z: m // h != z // h)
+    t2_part(start, far_part, (0, 1))
     if chunks == 2:
+        start_chunks(lambda m, z: m // h == z // h)
+        t2_part(start, 1 - far_part, (0, 1))
         left_copy = pltpu.make_async_copy(
             lf, packed.at[rows(me * sz.all + sz.main, sz.left), :], in_sem.at[0, 2]
         )
         left_copy.start()
-    for r in range(2):
-        for copy in t2_copies(info, t2, t2_v, t2_sem, r):
-            copy.start()
     packed[n * sz.all * TILE :, :] = jnp.zeros((TILE, TILE), BF16)
-    for z in range(n):
-        for c in range(chunks):
-            chunk_copy(own, z, c).wait()
-    if chunks == 2:
-        left_copy.wait()
-
-    def build(pair, to=b):
-        @pl.loop(0, n * sz.kd)
+    wait_chunks(far)
+
+    def build(pair, to, first, count):
+        @pl.loop(0, count * sz.kd)
         def _(k):
             for c in range(2):
-                tile = packed[rows(place[(2 * pair + c) * n * sz.kd + k]), :]
+                tile = packed[rows(place[((2 * pair + c) * n + first) * sz.kd + k]), :]
                 to[rows(k), c * TILE : (c + 1) * TILE] = tile
 
         return to
 
-    multiply(info[chunks], info[chunks + 1], build, info, t2, t2_v, t2_sem, out, held, out_sem)
+    deep = h * sz.kd * TILE
+    multiply(
+        info[chunks], jnp.minimum(info[chunks + 1], sz.sure),
+        lambda pair: build(pair, b.at[pl.ds(0, deep), :], far, h),
+        lambda rs: t2_part(wait, far_part, rs), t2_v, out, held, out_sem,
+        pl.ds(pl.multiple_of(far * sz.kd * TILE, deep), deep), acc, acc_v, acc_sem,
+    )
     if chunks == 2:
+        wait_chunks(h - far)
+        left_copy.wait()
+        t2_part(wait, 1 - far_part, (0, 1))
+        multiply(
+            jnp.int32(sz.sure), info[3], lambda pair: build(pair, b, 0, n),
+            lambda rs: None, t2_v, out, held, out_sem,
+        )
         for j in range(sz.pairs - sz.sure):
-            build(sz.sure + j, rest.at[j])
-
-
-def main_part(sz, chunks, info, place, t2, own, got, ends, lf=None, begun=None):
+            build(sz.sure + j, rest.at[j], 0, n)
+
+
+def early_kernel(sz, n_t2, here, place, *refs):
+    h = sz.near
+    t2, own, refs = refs[:n_t2], refs[n_t2], refs[n_t2 + 1 :]
+    got, refs = [refs[2 * s : 2 * s + 2] for s in range(h - 1)], refs[2 * (h - 1) :]
+    acc, packed, b, held, t2_v, in_sem, out_sem, t2_sem = refs
+    me, col = here[0], here[1]
+
+    def main_copy(ref, z):
+        to = packed.at[pl.ds(z % h * sz.main * TILE, sz.main * TILE), :]
+        return pltpu.make_async_copy(ref.at[pl.ds(NOTE, sz.main * TILE), :], to, in_sem.at[z % h])
+
+    from_source(sz, me, own, got, lambda z, ref: main_copy(ref, z).start(), lambda m, z: m // h == z // h)
+    part = me // h
+    t2_copies(start, col, part, t2, t2_v, t2_sem)
+    packed[h * sz.main * TILE :, :] = jnp.zeros((TILE, TILE), BF16)
+    for z in range(h):
+        main_copy(own, z).wait()
+
+    def build(pair):
+        @pl.loop(0, h * sz.kd)
+        def _(k):
+            for c in range(2):
+                tile = packed[rows(place[(2 * pair + c) * h * sz.kd + k]), :]
+                b[rows(k), c * TILE : (c + 1) * TILE] = tile
+
+        return b
+
+    deep = h * sz.kd * TILE
+    span = pl.ds(pl.multiple_of(jnp.where(me < h, 0, deep), deep), deep)
+    multiply(
+        jnp.int32(0), jnp.int32(sz.sure), build,
+        lambda rs: t2_copies(wait, col, part, t2, t2_v, t2_sem, rs), t2_v, acc, held, out_sem, span,
+    )
+
+
+def early_part(sz, here, place, t2, own, got):
+    ij, cd = t2[0].shape[0], t2[0].shape[1] * len(t2)
+    ops = [*t2, own, *(part for hop in got for part in hop)]
+    return pl.pallas_call(
+        functools.partial(early_kernel, sz, len(t2)),
+        out_shape=pltpu.HBM((sz.sure, ij, PAIR), jnp.float32),
+        in_specs=[SMEM, SMEM] + [ANY] * len(ops),
+        out_specs=HBM,
+        scratch_shapes=[
+            pltpu.VMEM(((sz.near * sz.main + 1) * TILE, TILE), BF16),
+            pltpu.VMEM((cd // 2, PAIR), BF16),
+            pltpu.VMEM((2, ij, PAIR), jnp.float32),
+            pltpu.VMEM((ij, cd), BF16),
+            pltpu.SemaphoreType.DMA((sz.near,)),
+            pltpu.SemaphoreType.DMA((2,)),
+            pltpu.SemaphoreType.DMA((len(t2), 2)),
+        ],
+        compiler_params=PARAMS,
+        cost_estimate=COST,
+        name="early_part",
+    )(here, place, *ops)
+
+
+def main_part(sz, chunks, info, place, t2, own, got, ends, acc, lf=None, begun=None):
     ij, cd = t2[0].shape[0], t2[0].shape[1] * len(t2)
     ops = [*t2, own, *(part for hop in got for part in hop), *ends[:chunks]]
     out_shape = [pltpu.HBM((ij, sz.nd * TILE), BF16)]
     aliases = {}
     if chunks == 2:
-        ops += [lf, begun]
+        ops += [lf, acc, begun]
         aliases = {2 + len(ops) - 1: 0}
         out_shape.append(jax.ShapeDtypeStruct((sz.pairs - sz.sure, cd, PAIR), BF16))
+        out_shape.append(pltpu.VMEM((ij, cd), BF16))
+    else:
+        ops += [acc]
     out = pl.pallas_call(
         functools.partial(main_kernel, sz, chunks, len(t2)),
         out_shape=out_shape,
         in_specs=[SMEM, SMEM] + [ANY] * len(ops),
-        out_specs=[HBM, VMEM][:chunks],
+        out_specs=[HBM, VMEM, VMEM][: 2 * chunks - 1],
         scratch_shapes=[
             pltpu.VMEM(((sz.n * sz.all + 1) * TILE, TILE), BF16),
             pltpu.VMEM((cd, PAIR), BF16),
             pltpu.VMEM((2, ij, PAIR), BF16),
-            pltpu.VMEM((ij, cd), BF16),
+            pltpu.VMEM((2, ij, PAIR), jnp.float32),
+            *([pltpu.VMEM((ij, cd), BF16)] if chunks == 1 else []),
             pltpu.SemaphoreType.DMA((sz.n, 3)),
+            pltpu.SemaphoreType.DMA((2,)),
             pltpu.SemaphoreType.DMA((2,)),
             pltpu.SemaphoreType.DMA((len(t2), 2)),
         ],
@@ -416,10 +582,9 @@
     return out if chunks == 2 else out[0]
 
 
-def tail_kernel(sz, n_t2, info, late, begun, rest, *refs):
+def tail_kernel(sz, info, late, begun, rest, t2_v, top_end, low_end, *refs):
     n, me = sz.n, info[0]
-    t2, (top_end, low_end, *refs) = refs[:n_t2], refs[n_t2:]
-    spread, (out, b, extra, held, t2_v, in_sem, out_sem, t2_sem) = refs[: n - 1], refs[n - 1 :]
+    spread, (out, b, extra, held, in_sem, out_sem) = refs[: n - 1], refs[n - 1 :]
     is_end = jnp.logical_or(me == 0, me == n - 1)
     size = sz.left * TILE
     from_top, from_low = (
@@ -440,9 +605,6 @@
                     act(copy)
 
     each(lambda copy: copy.start())
-    for r in range(2):
-        for copy in t2_copies(info, t2, t2_v, t2_sem, r):
-            copy.start()
     b[...] = rest[...]
     bases = []
     for z in range(n):
@@ -466,40 +628,38 @@
                             rows(bases[z] + p), :
                         ]
 
-    multiply(info[3], info[4], lambda pair: b.at[pair - sz.sure], info, t2, t2_v, t2_sem, out, held, out_sem)
-
-
-def tail_part(sz, info, late, t2, begun, rest, ends, spread):
-    ij, cd = t2[0].shape[0], t2[0].shape[1] * len(t2)
+    multiply(info[3], info[4], lambda pair: b.at[pair - sz.sure], lambda rs: None, t2_v, out, held, out_sem)
+
+
+def tail_part(sz, info, late, t2_v, begun, rest, ends, spread):
+    ij, cd = t2_v.shape
     pairs = sz.pairs - sz.sure
     region = max(ends[0].shape[0], (sz.n - 1) * sz.left * TILE)
     return pl.pallas_call(
-        functools.partial(tail_kernel, sz, len(t2)),
+        functools.partial(tail_kernel, sz),
         out_shape=pltpu.HBM(begun.shape, BF16),
-        in_specs=[SMEM, SMEM, HBM, VMEM] + [ANY] * (len(t2) + sz.n + 1),
+        in_specs=[SMEM, SMEM, HBM, VMEM, VMEM] + [ANY] * (sz.n + 1),
         out_specs=HBM,
         scratch_shapes=[
             pltpu.VMEM((pairs, cd, PAIR), BF16),
             pltpu.VMEM((region, TILE), BF16),
             pltpu.VMEM((2, ij, PAIR), BF16),
-            pltpu.VMEM((ij, cd), BF16),
             pltpu.SemaphoreType.DMA((sz.n - 1,)),
             pltpu.SemaphoreType.DMA((2,)),
-            pltpu.SemaphoreType.DMA((len(t2), 2)),
         ],
         input_output_aliases={2: 0},
         compiler_params=PARAMS,
         cost_estimate=COST,
         name="tail_part",
-    )(info, late, begun, rest, *t2, *ends, *spread)
-
-
-def last_hop(sz, length, info, place, late, t2, own, got, ends, lf, spread, begun):
+    )(info, late, begun, rest, t2_v, *ends, *spread)
+
+
+def last_hop(sz, length, info, place, late, t2, own, got, ends, acc, lf, spread, begun):
     n = sz.n
     joined = pool(sz, length, info, lf, spread)
     came = [lax.ppermute(joined, "row", pair) for pair in ([(n - 2, n - 1)], [(1, 0)])]
-    begun, rest = main_part(sz, 2, info, place, t2, own, got, ends, lf, begun)
-    return tail_part(sz, info, late, t2, begun, rest, came, spread)
+    begun, rest, t2_v = main_part(sz, 2, info, place, t2, own, got, ends, acc, lf, begun)
+    return tail_part(sz, info, late, t2_v, begun, rest, came, spread)
 
 
 def tie(value, after):
@@ -535,29 +695,31 @@
     ends = [(n - 2, n - 1), (1, 0)]
 
     def last(c, after):
-        return lax.ppermute(choose(sz, c, tie(here, after), *got[-1]), "row", ends)
+        return lax.ppermute(choose(sz, c, here, after, *got[-1]), "row", ends)
 
     def leftovers(d, after):
         pairs = [(i, i ^ d) for i in range(n) if 0 < i ^ d < n - 1]
         return lax.ppermute(tie(lf, after), "row", pairs)
 
     spread = {1: leftovers(1, got[0])}
-    first = last(0, (t2, spread[1]))
+    near = got[: sz.near - 1]
+    acc = early_part(sz, here, near_plan(sz, here, own, near), t2, own, near)
+    first = last(0, tie(here, (t2, spread[1], acc)))
     need = longest(sz, here, own, got)
     need = lax.pmax(need, "col")
     second = last(1, need)
     spread.update({d: leftovers(d, need) for d in range(2, n)})
     spread = [spread[d] for d in range(1, n)]
     place, late, info = plan(sz, tie(here, need), own, got, first)
-    told = lax.ppermute(tie(need, place), "row", ends)
-    need = jnp.where(jnp.logical_or(me == 0, me == n - 1), told, need)[0]
-    begun = main_part(sz, 1, info, place, t2, own, got, (first,))
+    begun = main_part(sz, 1, info, place, t2, own, got, (first,), acc)
+    is_end = jnp.logical_or(me == 0, me == n - 1)
+    need = jnp.where(is_end, tie(second, begun)[0, 0].astype(jnp.int32), need[0])
 
     branch = sum((need > length).astype(jnp.int32) for length in sz.lengths[:-1])
     return lax.switch(
         branch,
         [functools.partial(last_hop, sz, length) for length in sz.lengths],
-        info, place, late, t2, own, got, (first, second), lf, spread, begun,
+        info, place, late, t2, own, got, (first, second), acc, lf, spread, begun,
     )
 
 

time: 163 us -> 157 us (0.963)
  waiting for transfers between devices: 55.7 us -> 40.2 us
  Pallas kernels: 53.4 us -> 64.5 us
  starting transfers between devices: 40.8 us -> 37 us
    pallas_call x1 -> x3, Pallas kernels: 6.12 us -> 21 us  [the longest x1 13.4 us: early_part(): pl.pallas_call(functools.partial(early_kernel, sz, len(t2)), out_shape=pl...]
    ppermute x3, waiting for transfers between devices: 11.2 us -> 0.01 us  [leftovers(): return lax.ppermute(tie(lf, after), 'row', pairs)]
    ppermute x4, waiting for transfers between devices: 9.32 us -> 3.85 us  [hop(): return (lax.ppermute(up, 'row', pairs), lax.ppermute(down, 'row', back))]
    pallas_call x2, Pallas kernels: 30.8 us -> 26.9 us  [main_part(): pl.pallas_call(functools.partial(main_kernel, sz, chunks, len(t2)), out_s...]
    ppermute x3, starting transfers between devices: 17.2 us -> 14.8 us  [leftovers(): return lax.ppermute(tie(lf, after), 'row', pairs)]
    ppermute x3 -> x2, starting transfers between devices: 3.88 us -> 2.58 us  [last(): return lax.ppermute(choose(sz, c, here, after, *got[-1]), 'row', ends)]
  transfers between devices with their start and end apart: 19 -> 18, of which waited for: 5 -> 3; matrix products, arithmetic and copies ran while one was open for 0% -> 1% of each run, Pallas kernels for 25% -> 33%
where the time goes in v2:
time: 157 us; the launch traced here: 156 us
  Pallas kernels  64.5 us (41%)
  waiting for transfers between devices  40.2 us (26%)
  starting transfers between devices  37 us (24%)
  blocking collectives  8.63 us (5%)
  local copies, waits for them, and re-layouts  2.35 us (1%)
  between operations  1.73 us (1%)
    ppermute x7, waiting for transfers between devices, across(): return lax.ppermute(value, 'col', [(i, i ^ d) for i in range(n_col)])  36.3 us
    pallas_call x2, Pallas kernels, main_part(): pl.pallas_call(functools.partial(main_kernel, sz, chunks, len(t2)), out_s...  26.9 us
    ppermute x3, starting transfers between devices, leftovers(): return lax.ppermute(tie(lf, after), 'row', pairs)  14.8 us
    pallas_call x1, Pallas kernels, early_part(): pl.pallas_call(functools.partial(early_kernel, sz, len(t2)), out_shape=pl...  13.4 us
    ppermute x4, starting transfers between devices, hop(): return (lax.ppermute(up, 'row', pairs), lax.ppermute(down, 'row', back))  11.1 us
    pmax x1, blocking collectives, body(): need = lax.pmax(need, 'col')  8.63 us
    ppermute x7, starting transfers between devices, across(): return lax.ppermute(value, 'col', [(i, i ^ d) for i in range(n_col)])  6.56 us
    pallas_call x1, Pallas kernels, tail_part(): pl.pallas_call(functools.partial(tail_kernel, sz), out_shape=pltpu.HBM(be...  5.19 us
  transfers between devices with their start and end apart: 18, of which 3 were waited for; matrix products, arithmetic and copies ran while one was open for 1% of the time, Pallas kernels for 33%

profile of v2, /device:TPU:0, one launch (start us, length us, event | category | flops | bytes accessed | tf_op | source)
XLA Modules:
  0.0 155.8 jit_solution(645825651895363654)
XLA Ops:
  0.0 4.0 %begin.1 = (bf16[6160,128]{1,0:T(8,128)(2,1)S(1)}, bf16[2048,128]{1,0:T(8,128)(2,1)}, bf16[2048,256]{1,0:T(8,128)(2,1)}) custom-call(s32[4,16]{1,0:T(4,128)} %v_mask_hbm.1, s32[4,16]{1,0:T(4,128)} %v_mask_hbm.1, s32[2,16]{1,0:T(2,128)} %bitcast.6, bf16[512,2048]{1,0:T(8,128)(2,1)} %v.1, bf16[2048,256]{1,0:T(8,128)(2,1)} %t2.1), custom_call_target="tpu_custom_call" | custom-call | tf_op jit(solution)/shard_map/begin/pallas_call | solution.py:93
  4.0 1.3 collective-permute-start.15
  5.3 6.7 %collective-permute-start.14 = (bf16[6160,128]{1,0:T(8,128)(2,1)S(1)}, bf16[6160,128]{1,0:T(8,128)(2,1)}, u32[]{:S(2)}, u32[]{:S(2)}) collective-permute-start(bf16[6160,128]{1,0:T(8,128)(2,1)S(1)} %get-tuple-element.552.refs_0_.own.refs_8_), channel_id=1, source_target_pairs={{0,8},{8,16},{16,24},{1,9},{9,17},{17,25},{2,10},{10,18},{18,26},{... | collective-permute-start | bytes 4730888 | tf_op jit(solution)/shard_map/ppermute | solution.py:681
  12.0 1.9 %collective-permute-start.16 = (bf16[2048,256]{1,0:T(8,128)(2,1)}, bf16[2048,256]{1,0:T(8,128)(2,1)}, u32[]{:S(2)}, u32[]{:S(2)}) collective-permute-start(bf16[2048,256]{1,0:T(8,128)(2,1)} %get-tuple-element.557.refs_0_), channel_id=1, source_target_pairs={{0,2},{1,3},{2,0},{3,1},{4,6},{5,7},{6,4},{7,5},{8,10},{9,11},{10,... | collective-permute-start | bytes 3145736 | tf_op jit(solution)/shard_map/ppermute | solution.py:684
  13.9 1.5 collective-permute-start.17
  15.5 21.5 %collective-permute-done.16.refs_2_ = bf16[2048,256]{1,0:T(8,128)(2,1)} collective-permute-done((bf16[2048,256]{1,0:T(8,128)(2,1)}, bf16[2048,256]{1,0:T(8,128)(2,1)}, u32[]{:S(2)}, u32[]{:S(2)}) %collective-permute-start.16) | collective-permute-done | bytes 1048608 | tf_op jit(solution)/shard_map/ppermute | solution.py:684
  37.0 2.6 %collective-permute-start.24 = (bf16[2048,256]{1,0:T(8,128)(2,1)}, bf16[2048,256]{1,0:T(8,128)(2,1)}, u32[]{:S(2)}, u32[]{:S(2)}) collective-permute-start(bf16[2048,256]{1,0:T(8,128)(2,1)} %get-tuple-element.557.refs_0_), channel_id=1, source_target_pairs={{0,6},{1,7},{2,4},{3,5},{4,2},{5,3},{6,0},{7,1},{8,14},{9,15},{10,... | collective-permute-start | bytes 3145736 | tf_op jit(solution)/shard_map/ppermute | solution.py:684
  39.6 3.8 %collective-permute-done.15.refs_2_.refs_1_.refs_10_ = bf16[6160,128]{1,0:T(8,128)(2,1)S(1)} collective-permute-done((bf16[6160,128]{1,0:T(8,128)(2,1)S(1)}, bf16[6160,128]{1,0:T(8,128)(2,1)S(1)}, u32[]{:S(2)}, u32[]{:S(2)}) %collective-permute-start.15) | collective-permute-done | bytes 1576992 | tf_op jit(solution)/shard_map/ppermute | solution.py:681
  43.4 1.3 collective-permute-start.19
  44.7 1.8 %collective-permute-start.18 = (bf16[6160,128]{1,0:T(8,128)(2,1)}, bf16[6160,128]{1,0:T(8,128)(2,1)}, u32[]{:S(2)}, u32[]{:S(2)}) collective-permute-start(bf16[6160,128]{1,0:T(8,128)(2,1)} %collective-permute-done.14.refs_1_.refs_0_.refs_9_), channel_id=1, source_target_pairs={{8,16},{16,24},{9,17},{17,25},{10,18},{18,26},{11,19},{19,27},{12,... | collective-permute-start | bytes 4730888 | tf_op jit(solution)/shard_map/ppermute | solution.py:681
  47.1 14.8 %collective-permute-done.24.refs_6_ = bf16[2048,256]{1,0:T(8,128)(2,1)} collective-permute-done((bf16[2048,256]{1,0:T(8,128)(2,1)}, bf16[2048,256]{1,0:T(8,128)(2,1)}, u32[]{:S(2)}, u32[]{:S(2)}) %collective-permute-start.24) | collective-permute-done | bytes 1048608 | tf_op jit(solution)/shard_map/ppermute | solution.py:684
  61.9 3.1 %collective-permute-start.26 = (bf16[2048,128]{1,0:T(8,128)(2,1)}, bf16[2048,128]{1,0:T(8,128)(2,1)}, u32[]{:S(2)}, u32[]{:S(2)}) collective-permute-start(bf16[2048,128]{1,0:T(8,128)(2,1)} %get-tuple-element.564), channel_id=1, source_target_pairs={{0,8},{24,16},{1,9},{25,17},{2,10},{26,18},{3,11},{27,19},{4,12},{... | collective-permute-start | bytes 1572872 | tf_op jit(solution)/shard_map/ppermute | solution.py:702
  65.6 2.4 %near_plan.1.place = s32[96]{0:T(128)} custom-call(s32[2]{0:T(128)} %pad_add_fusion.here.need, bf16[6160,128]{1,0:T(8,128)(2,1)S(1)} %get-tuple-element.552.refs_0_.own.refs_8_, bf16[6160,128]{1,0:T(8,128)(2,1)} %collective-permute-done.14.refs_1_.refs_0_.refs_9_, bf16[6160,128]{1,0:T(8,128)(2,1)S(1)} %collective-permute-done.15.refs_2_.refs_1_.refs_10_), custom_call_target="tpu_custom_call" | custom-call | tf_op jit(solution)/shard_map/near_plan/pallas_call | solution.py:198
  68.0 0.6 copy-done
  69.2 13.4 %early_part.1.refs_14_ = f32[6,2048,256]{2,1,0:T(8,128)} custom-call(s32[2]{0:T(128)S(1)} %copy-done, s32[96]{0:T(128)S(1)} %copy-done.2, bf16[2048,256]{1,0:T(8,128)(2,1)} %get-tuple-element.557.refs_0_, bf16[2048,256]{1,0:T(8,128)(2,1)} %copy-done.6, bf16[2048,256]{1,0:T(8,128)(2,1)} %collective-permute-done.16.refs_2_, ...), custom_call_target="tpu_custom_call" | custom-call | flops 1048576 | bytes 4096 | tf_op jit(solution)/shard_map/early_part/pallas_call | solution.py:529
  82.7 1.7 %choose.3 = bf16[3600,128]{1,0:T(8,128)(2,1)S(1)} custom-call(s32[2]{0:T(128)S(1)} %copy-done, s32[2]{0:T(128)S(1)} %copy-done, bf16[6160,128]{1,0:T(8,128)(2,1)} %collective-permute-done.18.refs_3_.up.refs_11_, bf16[6160,128]{1,0:T(8,128)(2,1)} %collective-permute-done.19.refs_4_.down.refs_12_), custom_call_target="tpu_custom_call" | custom-call | tf_op jit(solution)/shard_map/choose/pallas_call | solution.py:296
  84.4 1.3 collective-permute-start.27
  85.7 2.1 %longest.1 = s32[1]{0:T(128)} custom-call(s32[2]{0:T(128)} %pad_add_fusion.here.need, bf16[6160,128]{1,0:T(8,128)(2,1)S(1)} %get-tuple-element.552.refs_0_.own.refs_8_, bf16[6160,128]{1,0:T(8,128)(2,1)} %collective-permute-done.14.refs_1_.refs_0_.refs_9_, bf16[6160,128]{1,0:T(8,128)(2,1)} %copy-done.3, ...), custom_call_target="tpu_custom_call" | custom-call | tf_op jit(solution)/shard_map/longest/pallas_call | solution.py:143
  87.8 8.6 %pmax.7.need = s32[1]{0:T(128)} all-reduce(s32[1]{0:T(128)} %longest.1), channel_id=1, replica_groups=mesh['row'=4,'col'=8] {'col'}, use_global_device_ids=true, to_apply=%region_0.0 | all-reduce | flops 1 | bytes 8 | tf_op jit(solution)/shard_map/pmax | solution.py:709
  96.4 2.3 %choose.2 = bf16[2576,128]{1,0:T(8,128)(2,1)S(1)} custom-call(s32[2]{0:T(128)S(1)} %copy-done.1, s32[1]{0:T(128)} %pmax.7.need, bf16[6160,128]{1,0:T(8,128)(2,1)} %collective-permute-done.18.refs_3_.up.refs_11_, bf16[6160,128]{1,0:T(8,128)(2,1)} %collective-permute-done.19.refs_4_.down.refs_12_), custom_call_target="tpu_custom_call" | custom-call | tf_op jit(solution)/shard_map/choose/pallas_call | solution.py:296
  98.7 1.3 collective-permute-start.20
  100.0 1.5 collective-permute-start.29
  101.5 10.2 %collective-permute-start.28 = (bf16[2048,128]{1,0:T(8,128)(2,1)}, bf16[2048,128]{1,0:T(8,128)(2,1)}, u32[]{:S(2)}, u32[]{:S(2)}) collective-permute-start(bf16[2048,128]{1,0:T(8,128)(2,1)} %get-tuple-element.564), channel_id=1, source_target_pairs={{0,16},{24,8},{1,17},{25,9},{2,18},{26,10},{3,19},{27,11},{4,20},{... | collective-permute-start | bytes 1572872 | tf_op jit(solution)/shard_map/ppermute | solution.py:702
  111.7 5.0 %plan.1 = (s32[256]{0:T(256)S(1)}, s32[256]{0:T(256)S(1)}, s32[10]{0:T(128)S(1)}) custom-call(s32[2]{0:T(128)} %pad_add_fusion.here.need, bf16[6160,128]{1,0:T(8,128)(2,1)S(1)} %get-tuple-element.552.refs_0_.own.refs_8_, bf16[6160,128]{1,0:T(8,128)(2,1)} %collective-permute-done.14.refs_1_.refs_0_.refs_9_, bf16[6160,128]{1,0:T(8,128)(2,1)} %copy-done.3, ...), custom_call_target="tpu_custom_call" | custom-call | tf_op jit(solution)/shard_map/plan/pallas_call | solution.py:261
  116.7 12.0 %main_part.15 = bf16[2048,2048]{1,0:T(8,128)(2,1)} custom-call(s32[10]{0:T(128)S(1)} %get-tuple-element.561.info, s32[256]{0:T(256)S(1)} %get-tuple-element.562.place, bf16[2048,256]{1,0:T(8,128)(2,1)S(1)} %copy-done.4, bf16[2048,256]{1,0:T(8,128)(2,1)} %copy-done.6, bf16[2048,256]{1,0:T(8,128)(2,1)} %collective-permute-done.16.refs_2_, ...), custom_call_target="tpu_custom_call" | custom-call | flops 1048576 | bytes 4096 | tf_op jit(solution)/shard_map/main_part/pallas_call | solution.py:561
  128.7 1.1 slice.3
  131.1 24.4 %conditional.1 = (bf16[2048,2048]{1,0:T(8,128)(2,1)}) conditional(s32[]{:T(128)} %clamp.3, (s32[10]{0:T(128)S(1)}, s32[256]{0:T(256)S(1)}, bf16[2048,256]{1,0:T(8,128)(2,1)S(1)}, bf16[2048,256]{1,0:T(8,128)(2,1)}, bf16[2048,256]{1,0:T(8,128)(2,1)}, /*index=5*/bf16[2048,256]{1,0:T(8,128)(2,1)}, ...), branch_computations={%region_1.2_spmd, %region_2.3_spmd, %region_3.4_spmd, %region_4.5_... | conditional | flops 2097152 | bytes 12591192 | solution.py:719
  131.4 1.5 pool.9
  132.9 1.3 collective-permute-start.5
  134.2 0.7 collective-permute-start.4
  134.9 14.9 %main_part.10 = (bf16[2048,2048]{1,0:T(8,128)(2,1)}, bf16[2,2048,256]{2,1,0:T(8,128)(2,1)S(1)}, bf16[2048,2048]{1,0:T(8,128)(2,1)S(1)}) custom-call(s32[10]{0:T(128)S(1)} %get-tuple-element.403.info, s32[256]{0:T(256)S(1)} %get-tuple-element.405.place, bf16[2048,256]{1,0:T(8,128)(2,1)S(1)} %get-tuple-element.406.refs_0_, ...), custom_call_target="tpu_custom_call", output_to_operand_aliasing={{0}: (19, {})} | custom-call | flops 1048576 | bytes 4096 | tf_op jit(solution)/shard_map/cond/branch_2_fun/main_part/pallas_call | solution.py:561
  149.9 5.2 %tail_part.9 = bf16[2048,2048]{1,0:T(8,128)(2,1)} custom-call(s32[10]{0:T(128)S(1)} %get-tuple-element.403.info, s32[256]{0:T(256)S(1)} %get-tuple-element.404.late, bf16[2048,2048]{1,0:T(8,128)(2,1)} %get-tuple-element.424.begun, bf16[2,2048,256]{2,1,0:T(8,128)(2,1)S(1)} %get-tuple-element.425.rest, ...), custom_call_target="tpu_custom_call", output_to_operand_aliasing={{}: (2, {})} | custom-call | flops 1048576 | bytes 4096 | tf_op jit(solution)/shard_map/cond/branch_2_fun/tail_part/pallas_call | solution.py:638
  (35 shorter events, 1.8 us)
Async XLA Ops:
  4.0 39.4 %collective-permute-start.15 = (bf16[6160,128]{1,0:T(8,128)(2,1)S(1)}, bf16[6160,128]{1,0:T(8,128)(2,1)S(1)}, u32[]{:S(2)}, u32[]{:S(2)}) collective-permute-start(bf16[6160,128]{1,0:T(8,128)(2,1)S(1)} %get-tuple-element.552.refs_0_.own.refs_8_), channel_id=1, source_target_pairs={{24,16},{16,8},{8,0},{25,17},{17,9},{9,1},{26,18},{18,10},{10,2},{... | collective-permute-start | bytes 4730888 | tf_op jit(solution)/shard_map/ppermute | solution.py:681
  5.3 39.4 %collective-permute-start.14 = (bf16[6160,128]{1,0:T(8,128)(2,1)S(1)}, bf16[6160,128]{1,0:T(8,128)(2,1)}, u32[]{:S(2)}, u32[]{:S(2)}) collective-permute-start(bf16[6160,128]{1,0:T(8,128)(2,1)S(1)} %get-tuple-element.552.refs_0_.own.refs_8_), channel_id=1, source_target_pairs={{0,8},{8,16},{16,24},{1,9},{9,17},{17,25},{2,10},{10,18},{18,26},{... | collective-permute-start | bytes 4730888 | tf_op jit(solution)/shard_map/ppermute | solution.py:681
  12.0 24.9 %collective-permute-start.16 = (bf16[2048,256]{1,0:T(8,128)(2,1)}, bf16[2048,256]{1,0:T(8,128)(2,1)}, u32[]{:S(2)}, u32[]{:S(2)}) collective-permute-start(bf16[2048,256]{1,0:T(8,128)(2,1)} %get-tuple-element.557.refs_0_), channel_id=1, source_target_pairs={{0,2},{1,3},{2,0},{3,1},{4,6},{5,7},{6,4},{7,5},{8,10},{9,11},{10,... | collective-permute-start | bytes 3145736 | tf_op jit(solution)/shard_map/ppermute | solution.py:684
  13.9 25.6 %collective-permute-start.17 = (bf16[2048,256]{1,0:T(8,128)(2,1)}, bf16[2048,256]{1,0:T(8,128)(2,1)S(1)}, u32[]{:S(2)}, u32[]{:S(2)}) collective-permute-start(bf16[2048,256]{1,0:T(8,128)(2,1)} %get-tuple-element.557.refs_0_), channel_id=1, source_target_pairs={{0,4},{1,5},{2,6},{3,7},{4,0},{5,1},{6,2},{7,3},{8,12},{9,13},{10,... | collective-permute-start | bytes 3145736 | tf_op jit(solution)/shard_map/ppermute | solution.py:684
  15.5 31.1 %collective-permute-start.21 = (bf16[2048,256]{1,0:T(8,128)(2,1)}, bf16[2048,256]{1,0:T(8,128)(2,1)S(1)}, u32[]{:S(2)}, u32[]{:S(2)}) collective-permute-start(bf16[2048,256]{1,0:T(8,128)(2,1)} %get-tuple-element.557.refs_0_), channel_id=1, source_target_pairs={{0,1},{1,0},{2,3},{3,2},{4,5},{5,4},{6,7},{7,6},{8,9},{9,8},{10,11... | collective-permute-start | bytes 3145736 | tf_op jit(solution)/shard_map/ppermute | solution.py:684
  37.0 24.9 %collective-permute-start.24 = (bf16[2048,256]{1,0:T(8,128)(2,1)}, bf16[2048,256]{1,0:T(8,128)(2,1)}, u32[]{:S(2)}, u32[]{:S(2)}) collective-permute-start(bf16[2048,256]{1,0:T(8,128)(2,1)} %get-tuple-element.557.refs_0_), channel_id=1, source_target_pairs={{0,6},{1,7},{2,4},{3,5},{4,2},{5,3},{6,0},{7,1},{8,14},{9,15},{10,... | collective-permute-start | bytes 3145736 | tf_op jit(solution)/shard_map/ppermute | solution.py:684
  39.6 7.0 %copy-start.5 = (bf16[2048,256]{1,0:T(8,128)(2,1)}, bf16[2048,256]{1,0:T(8,128)(2,1)S(1)}, u32[]{:S(2)}) copy-start(bf16[2048,256]{1,0:T(8,128)(2,1)S(1)} %collective-permute-done.17.refs_4_) | copy-start | bytes 3145732
  43.4 39.2 %copy-start.3 = (bf16[6160,128]{1,0:T(8,128)(2,1)}, bf16[6160,128]{1,0:T(8,128)(2,1)S(1)}, u32[]{:S(2)}) copy-start(bf16[6160,128]{1,0:T(8,128)(2,1)S(1)} %collective-permute-done.15.refs_2_.refs_1_.refs_10_) | copy-start | bytes 4730884
  43.4 39.2 %collective-permute-start.19 = (bf16[6160,128]{1,0:T(8,128)(2,1)S(1)}, bf16[6160,128]{1,0:T(8,128)(2,1)}, u32[]{:S(2)}, u32[]{:S(2)}) collective-permute-start(bf16[6160,128]{1,0:T(8,128)(2,1)S(1)} %collective-permute-done.15.refs_2_.refs_1_.refs_10_), channel_id=1, source_target_pairs={{16,8},{8,0},{17,9},{9,1},{18,10},{10,2},{19,11},{11,3},{20,12},{1... | collective-permute-start | bytes 4730888 | tf_op jit(solution)/shard_map/ppermute | solution.py:681
  44.7 37.9 %collective-permute-start.18 = (bf16[6160,128]{1,0:T(8,128)(2,1)}, bf16[6160,128]{1,0:T(8,128)(2,1)}, u32[]{:S(2)}, u32[]{:S(2)}) collective-permute-start(bf16[6160,128]{1,0:T(8,128)(2,1)} %collective-permute-done.14.refs_1_.refs_0_.refs_9_), channel_id=1, source_target_pairs={{8,16},{16,24},{9,17},{17,25},{10,18},{18,26},{11,19},{19,27},{12,... | collective-permute-start | bytes 4730888 | tf_op jit(solution)/shard_map/ppermute | solution.py:681
  46.6 15.3 %collective-permute-start.23 = (bf16[2048,256]{1,0:T(8,128)(2,1)S(1)}, bf16[2048,256]{1,0:T(8,128)(2,1)S(1)}, u32[]{:S(2)}, u32[]{:S(2)}) collective-permute-start(bf16[2048,256]{1,0:T(8,128)(2,1)S(1)} %collective-permute-done.17.refs_4_), channel_id=1, source_target_pairs={{0,1},{1,0},{2,3},{3,2},{4,5},{5,4},{6,7},{7,6},{8,9},{9,8},{10,11... | collective-permute-start | bytes 3145736 | tf_op jit(solution)/shard_map/ppermute | solution.py:684
  46.6 15.3 %copy-start.6 = (bf16[2048,256]{1,0:T(8,128)(2,1)}, bf16[2048,256]{1,0:T(8,128)(2,1)S(1)}, u32[]{:S(2)}) copy-start(bf16[2048,256]{1,0:T(8,128)(2,1)S(1)} %collective-permute-done.21.refs_1_) | copy-start | bytes 3145732
  46.6 21.4 %collective-permute-start.22 = (bf16[2048,256]{1,0:T(8,128)(2,1)}, bf16[2048,256]{1,0:T(8,128)(2,1)}, u32[]{:S(2)}, u32[]{:S(2)}) collective-permute-start(bf16[2048,256]{1,0:T(8,128)(2,1)} %collective-permute-done.16.refs_2_), channel_id=1, source_target_pairs={{0,1},{1,0},{2,3},{3,2},{4,5},{5,4},{6,7},{7,6},{8,9},{9,8},{10,11... | collective-permute-start | bytes 3145736 | tf_op jit(solution)/shard_map/ppermute | solution.py:684
  61.9 6.1 %collective-permute-start.25 = (bf16[2048,256]{1,0:T(8,128)(2,1)}, bf16[2048,256]{1,0:T(8,128)(2,1)}, u32[]{:S(2)}, u32[]{:S(2)}) collective-permute-start(bf16[2048,256]{1,0:T(8,128)(2,1)} %collective-permute-done.24.refs_6_), channel_id=1, source_target_pairs={{0,1},{1,0},{2,3},{3,2},{4,5},{5,4},{6,7},{7,6},{8,9},{9,8},{10,11... | collective-permute-start | bytes 3145736 | tf_op jit(solution)/shard_map/ppermute | solution.py:684
  61.9 3.1 %copy-start.7 = (bf16[2048,256]{1,0:T(8,128)(2,1)}, bf16[2048,256]{1,0:T(8,128)(2,1)S(1)}, u32[]{:S(2)}) copy-start(bf16[2048,256]{1,0:T(8,128)(2,1)S(1)} %collective-permute-done.23.refs_5_) | copy-start | bytes 3145732
  61.9 20.7 %collective-permute-start.26 = (bf16[2048,128]{1,0:T(8,128)(2,1)}, bf16[2048,128]{1,0:T(8,128)(2,1)}, u32[]{:S(2)}, u32[]{:S(2)}) collective-permute-start(bf16[2048,128]{1,0:T(8,128)(2,1)} %get-tuple-element.564), channel_id=1, source_target_pairs={{0,8},{24,16},{1,9},{25,17},{2,10},{26,18},{3,11},{27,19},{4,12},{... | collective-permute-start | bytes 1572872 | tf_op jit(solution)/shard_map/ppermute | solution.py:702
  68.0 0.6 copy-start
  68.6 0.6 copy-start.2
  82.6 13.8 %copy-start.1 = (s32[2]{0:T(128)S(1)}, s32[2]{0:T(128)}, u32[]{:S(2)}) copy-start(s32[2]{0:T(128)} %pad_add_fusion.here.need) | copy-start | bytes 28
  84.4 27.3 %collective-permute-start.27 = (bf16[3600,128]{1,0:T(8,128)(2,1)S(1)}, bf16[3600,128]{1,0:T(8,128)(2,1)}, u32[]{:S(2)}, u32[]{:S(2)}) collective-permute-start(bf16[3600,128]{1,0:T(8,128)(2,1)S(1)} %choose.3), channel_id=1, source_target_pairs={{16,24},{8,0},{17,25},{9,1},{18,26},{10,2},{19,27},{11,3},{20,28},... | collective-permute-start | bytes 2764808 | tf_op jit(solution)/shard_map/ppermute | solution.py:698
  98.7 30.0 %collective-permute-start.20 = (bf16[2576,128]{1,0:T(8,128)(2,1)S(1)}, bf16[2576,128]{1,0:T(8,128)(2,1)}, u32[]{:S(2)}, u32[]{:S(2)}) collective-permute-start(bf16[2576,128]{1,0:T(8,128)(2,1)S(1)} %choose.2), channel_id=1, source_target_pairs={{16,24},{8,0},{17,25},{9,1},{18,26},{10,2},{19,27},{11,3},{20,28},... | collective-permute-start | bytes 1978376 | tf_op jit(solution)/shard_map/ppermute | solution.py:698
  100.0 31.1 %collective-permute-start.29 = (bf16[2048,128]{1,0:T(8,128)(2,1)}, bf16[2048,128]{1,0:T(8,128)(2,1)}, u32[]{:S(2)}, u32[]{:S(2)}) collective-permute-start(bf16[2048,128]{1,0:T(8,128)(2,1)} %get-tuple-element.564), channel_id=1, source_target_pairs={{8,16},{16,8},{9,17},{17,9},{10,18},{18,10},{11,19},{19,11},{12,20... | collective-permute-start | bytes 1572872 | tf_op jit(solution)/shard_map/ppermute | solution.py:702
  101.5 29.6 %collective-permute-start.28 = (bf16[2048,128]{1,0:T(8,128)(2,1)}, bf16[2048,128]{1,0:T(8,128)(2,1)}, u32[]{:S(2)}, u32[]{:S(2)}) collective-permute-start(bf16[2048,128]{1,0:T(8,128)(2,1)} %get-tuple-element.564), channel_id=1, source_target_pairs={{0,16},{24,8},{1,17},{25,9},{2,18},{26,10},{3,19},{27,11},{4,20},{... | collective-permute-start | bytes 1572872 | tf_op jit(solution)/shard_map/ppermute | solution.py:702
  111.7 5.0 %copy-start.4 = (bf16[2048,256]{1,0:T(8,128)(2,1)S(1)}, bf16[2048,256]{1,0:T(8,128)(2,1)}, u32[]{:S(2)}) copy-start(bf16[2048,256]{1,0:T(8,128)(2,1)} %get-tuple-element.557.refs_0_) | copy-start | bytes 3145732
  132.9 16.9 %collective-permute-start.5 = (bf16[1536,128]{1,0:T(8,128)(2,1)S(1)}, bf16[1536,128]{1,0:T(8,128)(2,1)S(1)}, u32[]{:S(2)}, u32[]{:S(2)}) collective-permute-start(bf16[1536,128]{1,0:T(8,128)(2,1)S(1)} %pool.9), channel_id=1, source_target_pairs={{8,0},{9,1},{10,2},{11,3},{12,4},{13,5},{14,6},{15,7}} | collective-permute-start | bytes 1179656 | tf_op jit(solution)/shard_map/cond/branch_2_fun/ppermute | solution.py:660
  134.2 15.7 %collective-permute-start.4 = (bf16[1536,128]{1,0:T(8,128)(2,1)S(1)}, bf16[1536,128]{1,0:T(8,128)(2,1)S(1)}, u32[]{:S(2)}, u32[]{:S(2)}) collective-permute-start(bf16[1536,128]{1,0:T(8,128)(2,1)S(1)} %pool.9), channel_id=1, source_target_pairs={{16,24},{17,25},{18,26},{19,27},{20,28},{21,29},{22,30},{23,31}} | collective-permute-start | bytes 1179656 | tf_op jit(solution)/shard_map/cond/branch_2_fun/ppermute | solution.py:660

commit v3 on v2

--- a/solution.py
+++ b/solution.py
@@ -19,7 +19,7 @@
 PARAMS = pltpu.CompilerParams(vmem_limit_bytes=40 << 20)
 COST = pl.CostEstimate(flops=1 << 20, bytes_accessed=1 << 12, transcendentals=0)
 LENGTHS = (8, 10, 12, 14, 16, 20)
-FIRST = 28
+FIRST = 24
 
 
 def rows(tile, count=1):
@@ -138,21 +138,6 @@
     out[0] = jnp.maximum(to_up, to_down)
 
 
-def longest(sz, here, own, got):
-    ops = (own, *(part for hop in got for part in hop))
-    return pl.pallas_call(
-        functools.partial(need_kernel, sz),
-        out_shape=jax.ShapeDtypeStruct((1,), jnp.int32),
-        in_specs=[SMEM] + [ANY] * len(ops),
-        out_specs=SMEM,
-        scratch_shapes=[
-            pltpu.VMEM((len(ops), NOTE, TILE), BF16),
-            pltpu.SemaphoreType.DMA((len(ops),)),
-        ],
-        name="longest",
-    )(here, *ops)
-
-
 def from_source(sz, me, own, got, act, take=None):
     for m in range(sz.n):
 
@@ -182,9 +167,10 @@
 
     def column(c, counts):
         counts = list(counts)
+        keeps = [[masks[z * NOTE + k, c] > 0 for k in range(sz.kd)] for z in range(h)]
         for z in range(h):
             for k in range(sz.kd):
-                kept, p = masks[z * NOTE + k, c] > 0, counts[z]
+                kept, p = keeps[z][k], counts[z]
                 at = jnp.where(jnp.logical_and(kept, p < sz.main), z * sz.main + p, h * sz.main)
                 place[(c * h + z) * sz.kd + k] = at
                 counts[z] = p + kept.astype(jnp.int32)
@@ -231,11 +217,12 @@
 
     def column(c, carry):
         counts, firsts, seconds = (list(carry[i * n : (i + 1) * n]) for i in range(3))
+        keeps = [[masks[z * NOTE + k, c] > 0 for k in range(sz.kd)] for z in range(n)]
         for z in range(n):
             have = jnp.where(me == z, sz.all, sz.main)
             for k in range(sz.kd):
                 i = c * n * sz.kd + z * sz.kd + k
-                kept, p = masks[z * NOTE + k, c] > 0, counts[z]
+                kept, p = keeps[z][k], counts[z]
                 place[i] = jnp.where(jnp.logical_and(kept, p < have), z * sz.all + p, n * sz.all)
                 late[i] = jnp.where(jnp.logical_and(kept, p >= have), p - sz.main, -1)
                 counts[z] = p + kept.astype(jnp.int32)
@@ -304,6 +291,37 @@
     )(here, need, up, down)
 
 
+def first_kernel(sz, here, *refs):
+    parts, (out, need, notes, note_sem, sem) = refs[: 2 * sz.n - 3], refs[2 * sz.n - 3 :]
+    at = sz.cut(0)[2]
+    up, down = (pltpu.make_async_copy(x.at[at, :], out, sem) for x in parts[-2:])
+    mine = here[0] == sz.n - 2
+    pl.when(mine)(lambda: up.start())
+    pl.when(jnp.logical_not(mine))(lambda: down.start())
+    need_kernel(sz, here, *parts, need, notes, note_sem)
+    up.wait()
+
+
+def choose_first(sz, here, own, got):
+    ops = (own, *(part for hop in got for part in hop))
+    return pl.pallas_call(
+        functools.partial(first_kernel, sz),
+        out_shape=(
+            jax.ShapeDtypeStruct((sz.cut(0)[2].size, TILE), BF16),
+            jax.ShapeDtypeStruct((1,), jnp.int32),
+        ),
+        in_specs=[SMEM] + [ANY] * len(ops),
+        out_specs=(VMEM, SMEM),
+        scratch_shapes=[
+            pltpu.VMEM((len(ops), NOTE, TILE), BF16),
+            pltpu.SemaphoreType.DMA((len(ops),)),
+            pltpu.SemaphoreType.DMA,
+        ],
+        compiler_params=PARAMS,
+        name="choose_first",
+    )(here, *ops)
+
+
 def pool_kernel(sz, length, info, lf, *refs):
     n, me = sz.n, info[0]
     spread, (out, joined) = refs[: n - 1], refs[n - 1 :]
@@ -485,7 +503,10 @@
             lambda rs: None, t2_v, out, held, out_sem,
         )
         for j in range(sz.pairs - sz.sure):
-            build(sz.sure + j, rest.at[j], 0, n)
+
+            @pl.when(sz.sure + j >= info[3])
+            def _():
+                build(sz.sure + j, rest.at[j], 0, n)
 
 
 def early_kernel(sz, n_t2, here, place, *refs):
@@ -582,22 +603,19 @@
     return out if chunks == 2 else out[0]
 
 
-def tail_kernel(sz, info, late, begun, rest, t2_v, top_end, low_end, *refs):
-    n, me = sz.n, info[0]
+def tail_kernel(sz, info, late, begun, rest, t2_v, end, *refs):
+    n, me, whole = sz.n, info[0], info[3]
     spread, (out, b, extra, held, in_sem, out_sem) = refs[: n - 1], refs[n - 1 :]
     is_end = jnp.logical_or(me == 0, me == n - 1)
     size = sz.left * TILE
-    from_top, from_low = (
-        [pltpu.make_async_copy(end, extra.at[pl.ds(0, end.shape[0]), :], in_sem.at[0])]
-        for end in (top_end, low_end)
-    )
+    from_pool = [pltpu.make_async_copy(end, extra.at[pl.ds(0, end.shape[0]), :], in_sem.at[0])]
     direct = [
         pltpu.make_async_copy(part, extra.at[pl.ds(i * size, size), :], in_sem.at[i])
         for i, part in enumerate(spread)
     ]
 
     def each(act):
-        for which, copies in ((me == n - 1, from_top), (me == 0, from_low), (jnp.logical_not(is_end), direct)):
+        for which, copies in ((is_end, from_pool), (jnp.logical_not(is_end), direct)):
 
             @pl.when(which)
             def _():
@@ -605,7 +623,12 @@
                     act(copy)
 
     each(lambda copy: copy.start())
-    b[...] = rest[...]
+    for j in range(sz.pairs - sz.sure):
+
+        @pl.when(sz.sure + j >= whole)
+        def _():
+            b[j] = rest[j]
+
     bases = []
     for z in range(n):
         top = sum((info[LEFTS + y] for y in range(z + 1, n - 1)), jnp.int32(0))
@@ -615,30 +638,33 @@
 
     each(lambda copy: copy.wait())
     for j in range(sz.pairs - sz.sure):
-        for z in range(n):
-
-            @pl.loop(0, sz.kd)
-            def _(k):
-                for c in range(2):
-                    p = late[((2 * (sz.sure + j) + c) * n + z) * sz.kd + k]
-
-                    @pl.when(p >= 0)
-                    def _():
-                        b[j, rows(z * sz.kd + k), c * TILE : (c + 1) * TILE] = extra[
-                            rows(bases[z] + p), :
-                        ]
-
-    multiply(info[3], info[4], lambda pair: b.at[pair - sz.sure], lambda rs: None, t2_v, out, held, out_sem)
-
-
-def tail_part(sz, info, late, t2_v, begun, rest, ends, spread):
+
+        @pl.when(sz.sure + j >= whole)
+        def _():
+            for z in range(n):
+
+                @pl.loop(0, sz.kd)
+                def _(k):
+                    for c in range(2):
+                        p = late[((2 * (sz.sure + j) + c) * n + z) * sz.kd + k]
+
+                        @pl.when(p >= 0)
+                        def _():
+                            b[j, rows(z * sz.kd + k), c * TILE : (c + 1) * TILE] = extra[
+                                rows(bases[z] + p), :
+                            ]
+
+    multiply(whole, info[4], lambda pair: b.at[pair - sz.sure], lambda rs: None, t2_v, out, held, out_sem)
+
+
+def tail_part(sz, info, late, t2_v, begun, rest, end, spread):
     ij, cd = t2_v.shape
     pairs = sz.pairs - sz.sure
-    region = max(ends[0].shape[0], (sz.n - 1) * sz.left * TILE)
+    region = max(end.shape[0], (sz.n - 1) * sz.left * TILE)
     return pl.pallas_call(
         functools.partial(tail_kernel, sz),
         out_shape=pltpu.HBM(begun.shape, BF16),
-        in_specs=[SMEM, SMEM, HBM, VMEM, VMEM] + [ANY] * (sz.n + 1),
+        in_specs=[SMEM, SMEM, HBM, VMEM, VMEM] + [ANY] * sz.n,
         out_specs=HBM,
         scratch_shapes=[
             pltpu.VMEM((pairs, cd, PAIR), BF16),
@@ -651,13 +677,12 @@
         compiler_params=PARAMS,
         cost_estimate=COST,
         name="tail_part",
-    )(info, late, begun, rest, t2_v, *ends, *spread)
+    )(info, late, begun, rest, t2_v, end, *spread)
 
 
 def last_hop(sz, length, info, place, late, t2, own, got, ends, acc, lf, spread, begun):
     n = sz.n
-    joined = pool(sz, length, info, lf, spread)
-    came = [lax.ppermute(joined, "row", pair) for pair in ([(n - 2, n - 1)], [(1, 0)])]
+    came = lax.ppermute(pool(sz, length, info, lf, spread), "row", [(n - 2, n - 1), (1, 0)])
     begun, rest, t2_v = main_part(sz, 2, info, place, t2, own, got, ends, acc, lf, begun)
     return tail_part(sz, info, late, t2_v, begun, rest, came, spread)
 
@@ -687,27 +712,25 @@
     got = [hop(0, (own, own))]
     for d in range(2, n_col, 2):
         t2[d] = across(screened if d < 6 else tie(screened, t2[2]), d)
+    for s in range(1, n - 2):
+        got.append(hop(s, got[-1], (t2[2], t2[4]) if s == 1 else None))
+    near = got[: sz.near - 1]
+    near_place = near_plan(sz, here, own, near)
     for d in range(0, n_col, 2):
-        t2[d + 1] = across(t2[d], 1)
+        t2[d + 1] = across(tie(t2[d], near_place) if d == 4 else t2[d], 1)
     t2 = [t2[d] for d in range(n_col)]
-    for s in range(1, n - 2):
-        got.append(hop(s, got[-1], t2[2:5:2] if s == 1 else None))
     ends = [(n - 2, n - 1), (1, 0)]
-
-    def last(c, after):
-        return lax.ppermute(choose(sz, c, here, after, *got[-1]), "row", ends)
 
     def leftovers(d, after):
         pairs = [(i, i ^ d) for i in range(n) if 0 < i ^ d < n - 1]
         return lax.ppermute(tie(lf, after), "row", pairs)
 
     spread = {1: leftovers(1, got[0])}
-    near = got[: sz.near - 1]
-    acc = early_part(sz, here, near_plan(sz, here, own, near), t2, own, near)
-    first = last(0, tie(here, (t2, spread[1], acc)))
-    need = longest(sz, here, own, got)
+    acc = early_part(sz, here, near_place, t2, own, near)
+    first, need = choose_first(sz, tie(here, (t2, spread[1], acc)), own, got)
+    first = lax.ppermute(first, "row", ends)
     need = lax.pmax(need, "col")
-    second = last(1, need)
+    second = lax.ppermute(choose(sz, 1, here, need, *got[-1]), "row", ends)
     spread.update({d: leftovers(d, need) for d in range(2, n)})
     spread = [spread[d] for d in range(1, n)]
     place, late, info = plan(sz, tie(here, need), own, got, first)

time: 157 us -> 156 us (level); the launches traced: 156 us -> 153 us
  starting transfers between devices: 37 us -> 30.1 us
  waiting for transfers between devices: 40.2 us -> 45.3 us
    ppermute x4, waiting for transfers between devices: 3.85 us -> 13.4 us  [hop(): return (lax.ppermute(up, 'row', pairs), lax.ppermute(down, 'row', back))]
    ppermute x7, waiting for transfers between devices: 36.3 us -> 29.6 us  [across(): return lax.ppermute(value, 'col', [(i, i ^ d) for i in range(n_col)])]
    ppermute x3, starting transfers between devices: 14.8 us -> 10.7 us  [leftovers(): return lax.ppermute(tie(lf, after), 'row', pairs)]
    ppermute x4 -> x3, waiting for transfers between devices: 0.01 us -> 2.24 us  [the longest x1 2.24 us: body(): first = lax.ppermute(first, 'row', ends)]
    ppermute x4, starting transfers between devices: 11.1 us -> 9.4 us  [hop(): return (lax.ppermute(up, 'row', pairs), lax.ppermute(down, 'row', back))]
    pallas_call x2 -> x1, Pallas kernels: 4.06 us -> 2.38 us  [choose(): pl.pallas_call(functools.partial(choose_kernel, sz, c), out_shape=jax.Sha...]
    ppermute x4 -> x3, starting transfers between devices: 4.56 us -> 3.88 us  [the longest x1 1.29 us: last_hop(): lax.ppermute(pool(sz, length, info, lf, spread), 'row', [(n - 2, n - 1),...]
  transfers between devices with their start and end apart: 18 -> 17, of which waited for: 3 -> 6; matrix products, arithmetic and copies ran while one was open for 1% -> 1% of each run, Pallas kernels for 33% -> 33%
where the time goes in v3:
time: 156 us; the launch traced here: 153 us
  Pallas kernels  63.1 us (40%)
  waiting for transfers between devices  45.3 us (29%)
  starting transfers between devices  30.1 us (19%)
  blocking collectives  8.63 us (6%)
  local copies, waits for them, and re-layouts  2.49 us (2%)
  between operations  1.86 us (1%)
    ppermute x7, waiting for transfers between devices, across(): return lax.ppermute(value, 'col', [(i, i ^ d) for i in range(n_col)])  29.6 us
    pallas_call x2, Pallas kernels, main_part(): pl.pallas_call(functools.partial(main_kernel, sz, chunks, len(t2)), out_s...  26.8 us
    pallas_call x1, Pallas kernels, early_part(): pl.pallas_call(functools.partial(early_kernel, sz, len(t2)), out_shape=pl...  13.7 us
    ppermute x4, waiting for transfers between devices, hop(): return (lax.ppermute(up, 'row', pairs), lax.ppermute(down, 'row', back))  13.4 us
    ppermute x3, starting transfers between devices, leftovers(): return lax.ppermute(tie(lf, after), 'row', pairs)  10.7 us
    ppermute x4, starting transfers between devices, hop(): return (lax.ppermute(up, 'row', pairs), lax.ppermute(down, 'row', back))  9.4 us
    pmax x1, blocking collectives, body(): need = lax.pmax(need, 'col')  8.63 us
    ppermute x7, starting transfers between devices, across(): return lax.ppermute(value, 'col', [(i, i ^ d) for i in range(n_col)])  6.15 us
  transfers between devices with their start and end apart: 17, of which 6 were waited for; matrix products, arithmetic and copies ran while one was open for 1% of the time, Pallas kernels for 33%

profile of v3, /device:TPU:0, one launch (start us, length us, event | category | flops | bytes accessed | tf_op | source)
XLA Modules:
  0.0 152.9 jit_solution(10428283842276456311)
XLA Ops:
  0.0 4.0 %begin.1 = (bf16[6160,128]{1,0:T(8,128)(2,1)S(1)}, bf16[2048,128]{1,0:T(8,128)(2,1)}, bf16[2048,256]{1,0:T(8,128)(2,1)}) custom-call(s32[4,16]{1,0:T(4,128)} %v_mask_hbm.1, s32[4,16]{1,0:T(4,128)} %v_mask_hbm.1, s32[2,16]{1,0:T(2,128)} %bitcast.6, bf16[512,2048]{1,0:T(8,128)(2,1)} %v.1, bf16[2048,256]{1,0:T(8,128)(2,1)} %t2.1), custom_call_target="tpu_custom_call" | custom-call | tf_op jit(solution)/shard_map/begin/pallas_call | solution.py:93
  4.0 5.0 %collective-permute-start.11 = (bf16[6160,128]{1,0:T(8,128)(2,1)S(1)}, bf16[6160,128]{1,0:T(8,128)(2,1)S(1)}, u32[]{:S(2)}, u32[]{:S(2)}) collective-permute-start(bf16[6160,128]{1,0:T(8,128)(2,1)S(1)} %get-tuple-element.556.own.refs_8_.refs_0_), channel_id=1, source_target_pairs={{0,8},{8,16},{16,24},{1,9},{9,17},{17,25},{2,10},{10,18},{18,26},{... | collective-permute-start | bytes 4730888 | tf_op jit(solution)/shard_map/ppermute | solution.py:706
  9.0 1.3 collective-permute-start.12
  10.3 1.6 %collective-permute-start.8 = (bf16[2048,256]{1,0:T(8,128)(2,1)}, bf16[2048,256]{1,0:T(8,128)(2,1)}, u32[]{:S(2)}, u32[]{:S(2)}) collective-permute-start(bf16[2048,256]{1,0:T(8,128)(2,1)} %get-tuple-element.558.refs_0_), channel_id=1, source_target_pairs={{0,2},{1,3},{2,0},{3,1},{4,6},{5,7},{6,4},{7,5},{8,10},{9,11},{10,... | collective-permute-start | bytes 3145736 | tf_op jit(solution)/shard_map/ppermute | solution.py:709
  11.9 1.5 collective-permute-start.10
  13.4 21.9 %collective-permute-done.8.refs_2_ = bf16[2048,256]{1,0:T(8,128)(2,1)} collective-permute-done((bf16[2048,256]{1,0:T(8,128)(2,1)}, bf16[2048,256]{1,0:T(8,128)(2,1)}, u32[]{:S(2)}, u32[]{:S(2)}) %collective-permute-start.8) | collective-permute-done | bytes 1048608 | tf_op jit(solution)/shard_map/ppermute | solution.py:709
  35.3 2.4 %collective-permute-start.14 = (bf16[2048,256]{1,0:T(8,128)(2,1)}, bf16[2048,256]{1,0:T(8,128)(2,1)}, u32[]{:S(2)}, u32[]{:S(2)}) collective-permute-start(bf16[2048,256]{1,0:T(8,128)(2,1)} %get-tuple-element.558.refs_0_), channel_id=1, source_target_pairs={{0,6},{1,7},{2,4},{3,5},{4,2},{5,3},{6,0},{7,1},{8,14},{9,15},{10,... | collective-permute-start | bytes 3145736 | tf_op jit(solution)/shard_map/ppermute | solution.py:709
  37.8 4.9 %collective-permute-done.11.refs_0_.refs_9_.refs_1_ = bf16[6160,128]{1,0:T(8,128)(2,1)S(1)} collective-permute-done((bf16[6160,128]{1,0:T(8,128)(2,1)S(1)}, bf16[6160,128]{1,0:T(8,128)(2,1)S(1)}, u32[]{:S(2)}, u32[]{:S(2)}) %collective-permute-start.11) | collective-permute-done | bytes 1576992 | tf_op jit(solution)/shard_map/ppermute | solution.py:706
  42.7 1.8 %collective-permute-start.17 = (bf16[6160,128]{1,0:T(8,128)(2,1)S(1)}, bf16[6160,128]{1,0:T(8,128)(2,1)}, u32[]{:S(2)}, u32[]{:S(2)}) collective-permute-start(bf16[6160,128]{1,0:T(8,128)(2,1)S(1)} %collective-permute-done.11.refs_0_.refs_9_.refs_1_), channel_id=1, source_target_pairs={{8,16},{16,24},{9,17},{17,25},{10,18},{18,26},{11,19},{19,27},{12,... | collective-permute-start | bytes 4730888 | tf_op jit(solution)/shard_map/ppermute | solution.py:706
  44.5 2.5 %collective-permute-done.12.refs_1_.refs_10_.refs_2_ = bf16[6160,128]{1,0:T(8,128)(2,1)} collective-permute-done((bf16[6160,128]{1,0:T(8,128)(2,1)S(1)}, bf16[6160,128]{1,0:T(8,128)(2,1)}, u32[]{:S(2)}, u32[]{:S(2)}) %collective-permute-start.12) | collective-permute-done | bytes 1576992 | tf_op jit(solution)/shard_map/ppermute | solution.py:706
  47.0 1.3 collective-permute-start.18
  49.0 3.1 %near_plan.1.place = s32[96]{0:T(128)} custom-call(s32[2]{0:T(128)} %pad_add_fusion.here, bf16[6160,128]{1,0:T(8,128)(2,1)S(1)} %get-tuple-element.556.own.refs_8_.refs_0_, bf16[6160,128]{1,0:T(8,128)(2,1)S(1)} %collective-permute-done.11.refs_0_.refs_9_.refs_1_, bf16[6160,128]{1,0:T(8,128)(2,1)} %collective-permute-done.12.refs_1_.refs_10_.refs_2_), custom_call_target="tpu_custom_call" | custom-call | tf_op jit(solution)/shard_map/near_plan/pallas_call | solution.py:184
  52.6 7.7 %collective-permute-done.14.refs_6_ = bf16[2048,256]{1,0:T(8,128)(2,1)} collective-permute-done((bf16[2048,256]{1,0:T(8,128)(2,1)}, bf16[2048,256]{1,0:T(8,128)(2,1)}, u32[]{:S(2)}, u32[]{:S(2)}) %collective-permute-start.14) | collective-permute-done | bytes 1048608 | tf_op jit(solution)/shard_map/ppermute | solution.py:709
  60.3 4.0 %collective-permute-start.16 = (bf16[2048,128]{1,0:T(8,128)(2,1)}, bf16[2048,128]{1,0:T(8,128)(2,1)S(1)}, u32[]{:S(2)}, u32[]{:S(2)}) collective-permute-start(bf16[2048,128]{1,0:T(8,128)(2,1)} %get-tuple-element.570), channel_id=1, source_target_pairs={{0,8},{24,16},{1,9},{25,17},{2,10},{26,18},{3,11},{27,19},{4,12},{... | collective-permute-start | bytes 1572872 | tf_op jit(solution)/shard_map/ppermute | solution.py:726
  65.6 13.7 %early_part.1.refs_14_ = f32[6,2048,256]{2,1,0:T(8,128)} custom-call(s32[2]{0:T(128)S(1)} %copy-done, s32[96]{0:T(128)S(1)} %copy-done.2, bf16[2048,256]{1,0:T(8,128)(2,1)} %get-tuple-element.558.refs_0_, bf16[2048,256]{1,0:T(8,128)(2,1)} %collective-permute-done.7.refs_1_, bf16[2048,256]{1,0:T(8,128)(2,1)} %collective-permute-done.8.refs_2_, ...), custom_call_target="tpu_custom_call" | custom-call | flops 1048576 | bytes 4096 | tf_op jit(solution)/shard_map/early_part/pallas_call | solution.py:550
  79.4 6.1 %collective-permute-done.18.refs_4_.down.refs_12_ = bf16[6160,128]{1,0:T(8,128)(2,1)} collective-permute-done((bf16[6160,128]{1,0:T(8,128)(2,1)}, bf16[6160,128]{1,0:T(8,128)(2,1)}, u32[]{:S(2)}, u32[]{:S(2)}) %collective-permute-start.18) | collective-permute-done | bytes 1576992 | tf_op jit(solution)/shard_map/ppermute | solution.py:706
  85.4 2.3 %choose_first.1 = (bf16[3088,128]{1,0:T(8,128)(2,1)S(1)}, s32[1]{0:T(128)}) custom-call(s32[2]{0:T(128)S(1)} %copy-done, bf16[6160,128]{1,0:T(8,128)(2,1)S(1)} %get-tuple-element.556.own.refs_8_.refs_0_, bf16[6160,128]{1,0:T(8,128)(2,1)} %copy-done.3, bf16[6160,128]{1,0:T(8,128)(2,1)} %collective-permute-done.12.refs_1_.refs_10_.refs_2_, ...), custom_call_target="tpu_custom_call" | custom-call | tf_op jit(solution)/shard_map/choose_first/pallas_call | solution.py:307
  87.7 1.3 collective-permute-start.20
  89.0 8.6 %pmax.7.need = s32[1]{0:T(128)} all-reduce(s32[1]{0:T(128)} %get-tuple-element.564), channel_id=1, replica_groups=mesh['row'=4,'col'=8] {'col'}, use_global_device_ids=true, to_apply=%region_0.0 | all-reduce | flops 1 | bytes 8 | tf_op jit(solution)/shard_map/pmax | solution.py:732
  97.6 2.4 %choose.1 = bf16[3088,128]{1,0:T(8,128)(2,1)S(1)} custom-call(s32[2]{0:T(128)S(1)} %copy-done.1, s32[1]{0:T(128)} %pmax.7.need, bf16[6160,128]{1,0:T(8,128)(2,1)} %collective-permute-done.17.refs_3_.up.refs_11_, bf16[6160,128]{1,0:T(8,128)(2,1)} %collective-permute-done.18.refs_4_.down.refs_12_), custom_call_target="tpu_custom_call" | custom-call | tf_op jit(solution)/shard_map/choose/pallas_call | solution.py:283
  100.0 1.3 collective-permute-start.19
  101.3 5.2 %collective-permute-start.21 = (bf16[2048,128]{1,0:T(8,128)(2,1)}, bf16[2048,128]{1,0:T(8,128)(2,1)}, u32[]{:S(2)}, u32[]{:S(2)}) collective-permute-start(bf16[2048,128]{1,0:T(8,128)(2,1)} %get-tuple-element.570), channel_id=1, source_target_pairs={{0,16},{24,8},{1,17},{25,9},{2,18},{26,10},{3,19},{27,11},{4,20},{... | collective-permute-start | bytes 1572872 | tf_op jit(solution)/shard_map/ppermute | solution.py:726
  106.6 1.5 collective-permute-start.22
  108.0 2.2 %collective-permute-done.20.refs_5_.refs_13_ = bf16[3088,128]{1,0:T(8,128)(2,1)} collective-permute-done((bf16[3088,128]{1,0:T(8,128)(2,1)S(1)}, bf16[3088,128]{1,0:T(8,128)(2,1)}, u32[]{:S(2)}, u32[]{:S(2)}) %collective-permute-start.20) | collective-permute-done | bytes 790560 | tf_op jit(solution)/shard_map/ppermute | solution.py:731
  110.3 4.9 %plan.1 = (s32[256]{0:T(256)S(1)}, s32[256]{0:T(256)S(1)}, s32[10]{0:T(128)S(1)}) custom-call(s32[2]{0:T(128)} %pad_add_fusion.here, bf16[6160,128]{1,0:T(8,128)(2,1)S(1)} %get-tuple-element.556.own.refs_8_.refs_0_, bf16[6160,128]{1,0:T(8,128)(2,1)} %copy-done.3, bf16[6160,128]{1,0:T(8,128)(2,1)} %collective-permute-done.12.refs_1_.refs_10_.refs_2_, ...), custom_call_target="tpu_custom_call" | custom-call | tf_op jit(solution)/shard_map/plan/pallas_call | solution.py:248
  115.2 10.3 %main_part.15 = bf16[2048,2048]{1,0:T(8,128)(2,1)} custom-call(s32[10]{0:T(128)S(1)} %get-tuple-element.567.info, s32[256]{0:T(256)S(1)} %get-tuple-element.568.place, bf16[2048,256]{1,0:T(8,128)(2,1)} %get-tuple-element.558.refs_0_, bf16[2048,256]{1,0:T(8,128)(2,1)} %collective-permute-done.7.refs_1_, bf16[2048,256]{1,0:T(8,128)(2,1)} %collective-permute-done.8.refs_2_, ...), custom_call_target="tpu_custom_call" | custom-call | flops 1048576 | bytes 4096 | tf_op jit(solution)/shard_map/main_part/pallas_call | solution.py:582
  125.5 1.2 slice.3
  128.1 24.6 %conditional.1 = (bf16[2048,2048]{1,0:T(8,128)(2,1)}) conditional(s32[]{:T(128)} %clamp.3, (s32[10]{0:T(128)S(1)}, s32[256]{0:T(256)S(1)}, bf16[2048,256]{1,0:T(8,128)(2,1)}, bf16[2048,256]{1,0:T(8,128)(2,1)}, bf16[2048,256]{1,0:T(8,128)(2,1)}, /*index=5*/bf16[2048,256]{1,0:T(8,128)(2,1)}, ...), branch_computations={%region_1.2_spmd, %region_2.3_spmd, %region_3.4_spmd, %region_4.5_... | conditional | flops 2097152 | bytes 6299696 | solution.py:742
  128.3 1.2 pool.9
  129.6 1.3 collective-permute-start.2
  130.9 16.5 %main_part.10 = (bf16[2048,2048]{1,0:T(8,128)(2,1)}, bf16[2,2048,256]{2,1,0:T(8,128)(2,1)S(1)}, bf16[2048,2048]{1,0:T(8,128)(2,1)S(1)}) custom-call(s32[10]{0:T(128)S(1)} %get-tuple-element.403.info, s32[256]{0:T(256)S(1)} %get-tuple-element.405.place, bf16[2048,256]{1,0:T(8,128)(2,1)} %get-tuple-element.406.refs_0_, ...), custom_call_target="tpu_custom_call", output_to_operand_aliasing={{0}: (19, {})} | custom-call | flops 1048576 | bytes 4096 | tf_op jit(solution)/shard_map/cond/branch_2_fun/main_part/pallas_call | solution.py:582
  147.4 4.8 %tail_part.9 = bf16[2048,2048]{1,0:T(8,128)(2,1)} custom-call(s32[10]{0:T(128)S(1)} %get-tuple-element.403.info, s32[256]{0:T(256)S(1)} %get-tuple-element.404.late, bf16[2048,2048]{1,0:T(8,128)(2,1)} %get-tuple-element.424.begun, bf16[2,2048,256]{2,1,0:T(8,128)(2,1)S(1)} %get-tuple-element.425.rest, ...), custom_call_target="tpu_custom_call", output_to_operand_aliasing={{}: (2, {})} | custom-call | flops 1048576 | bytes 4096 | tf_op jit(solution)/shard_map/cond/branch_2_fun/tail_part/pallas_call | solution.py:664
  (36 shorter events, 2.5 us)
Async XLA Ops:
  4.0 38.7 %collective-permute-start.11 = (bf16[6160,128]{1,0:T(8,128)(2,1)S(1)}, bf16[6160,128]{1,0:T(8,128)(2,1)S(1)}, u32[]{:S(2)}, u32[]{:S(2)}) collective-permute-start(bf16[6160,128]{1,0:T(8,128)(2,1)S(1)} %get-tuple-element.556.own.refs_8_.refs_0_), channel_id=1, source_target_pairs={{0,8},{8,16},{16,24},{1,9},{9,17},{17,25},{2,10},{10,18},{18,26},{... | collective-permute-start | bytes 4730888 | tf_op jit(solution)/shard_map/ppermute | solution.py:706
  9.0 37.9 %collective-permute-start.12 = (bf16[6160,128]{1,0:T(8,128)(2,1)S(1)}, bf16[6160,128]{1,0:T(8,128)(2,1)}, u32[]{:S(2)}, u32[]{:S(2)}) collective-permute-start(bf16[6160,128]{1,0:T(8,128)(2,1)S(1)} %get-tuple-element.556.own.refs_8_.refs_0_), channel_id=1, source_target_pairs={{24,16},{16,8},{8,0},{25,17},{17,9},{9,1},{26,18},{18,10},{10,2},{... | collective-permute-start | bytes 4730888 | tf_op jit(solution)/shard_map/ppermute | solution.py:706
  10.3 25.0 %collective-permute-start.8 = (bf16[2048,256]{1,0:T(8,128)(2,1)}, bf16[2048,256]{1,0:T(8,128)(2,1)}, u32[]{:S(2)}, u32[]{:S(2)}) collective-permute-start(bf16[2048,256]{1,0:T(8,128)(2,1)} %get-tuple-element.558.refs_0_), channel_id=1, source_target_pairs={{0,2},{1,3},{2,0},{3,1},{4,6},{5,7},{6,4},{7,5},{8,10},{9,11},{10,... | collective-permute-start | bytes 3145736 | tf_op jit(solution)/shard_map/ppermute | solution.py:709
  11.9 25.9 %collective-permute-start.10 = (bf16[2048,256]{1,0:T(8,128)(2,1)}, bf16[2048,256]{1,0:T(8,128)(2,1)S(1)}, u32[]{:S(2)}, u32[]{:S(2)}) collective-permute-start(bf16[2048,256]{1,0:T(8,128)(2,1)} %get-tuple-element.558.refs_0_), channel_id=1, source_target_pairs={{0,4},{1,5},{2,6},{3,7},{4,0},{5,1},{6,2},{7,3},{8,12},{9,13},{10,... | collective-permute-start | bytes 3145736 | tf_op jit(solution)/shard_map/ppermute | solution.py:709
  13.4 38.6 %collective-permute-start.7 = (bf16[2048,256]{1,0:T(8,128)(2,1)}, bf16[2048,256]{1,0:T(8,128)(2,1)}, u32[]{:S(2)}, u32[]{:S(2)}) collective-permute-start(bf16[2048,256]{1,0:T(8,128)(2,1)} %get-tuple-element.558.refs_0_), channel_id=1, source_target_pairs={{0,1},{1,0},{2,3},{3,2},{4,5},{5,4},{6,7},{7,6},{8,9},{9,8},{10,11... | collective-permute-start | bytes 3145736 | tf_op jit(solution)/shard_map/ppermute | solution.py:709
  35.3 24.9 %collective-permute-start.14 = (bf16[2048,256]{1,0:T(8,128)(2,1)}, bf16[2048,256]{1,0:T(8,128)(2,1)}, u32[]{:S(2)}, u32[]{:S(2)}) collective-permute-start(bf16[2048,256]{1,0:T(8,128)(2,1)} %get-tuple-element.558.refs_0_), channel_id=1, source_target_pairs={{0,6},{1,7},{2,4},{3,5},{4,2},{5,3},{6,0},{7,1},{8,14},{9,15},{10,... | collective-permute-start | bytes 3145736 | tf_op jit(solution)/shard_map/ppermute | solution.py:709
  37.8 9.2 %copy-start.7 = (bf16[2048,256]{1,0:T(8,128)(2,1)}, bf16[2048,256]{1,0:T(8,128)(2,1)S(1)}, u32[]{:S(2)}) copy-start(bf16[2048,256]{1,0:T(8,128)(2,1)S(1)} %collective-permute-done.10.refs_4_) | copy-start | bytes 3145732
  42.7 36.6 %copy-start.3 = (bf16[6160,128]{1,0:T(8,128)(2,1)}, bf16[6160,128]{1,0:T(8,128)(2,1)S(1)}, u32[]{:S(2)}) copy-start(bf16[6160,128]{1,0:T(8,128)(2,1)S(1)} %collective-permute-done.11.refs_0_.refs_9_.refs_1_) | copy-start | bytes 4730884
  42.7 36.7 %collective-permute-start.17 = (bf16[6160,128]{1,0:T(8,128)(2,1)S(1)}, bf16[6160,128]{1,0:T(8,128)(2,1)}, u32[]{:S(2)}, u32[]{:S(2)}) collective-permute-start(bf16[6160,128]{1,0:T(8,128)(2,1)S(1)} %collective-permute-done.11.refs_0_.refs_9_.refs_1_), channel_id=1, source_target_pairs={{8,16},{16,24},{9,17},{17,25},{10,18},{18,26},{11,19},{19,27},{12,... | collective-permute-start | bytes 4730888 | tf_op jit(solution)/shard_map/ppermute | solution.py:706
  47.0 38.4 %collective-permute-start.18 = (bf16[6160,128]{1,0:T(8,128)(2,1)}, bf16[6160,128]{1,0:T(8,128)(2,1)}, u32[]{:S(2)}, u32[]{:S(2)}) collective-permute-start(bf16[6160,128]{1,0:T(8,128)(2,1)} %collective-permute-done.12.refs_1_.refs_10_.refs_2_), channel_id=1, source_target_pairs={{16,8},{8,0},{17,9},{9,1},{18,10},{10,2},{19,11},{11,3},{20,12},{1... | collective-permute-start | bytes 4730888 | tf_op jit(solution)/shard_map/ppermute | solution.py:706
  48.3 12.0 %collective-permute-start.9 = (bf16[2048,256]{1,0:T(8,128)(2,1)}, bf16[2048,256]{1,0:T(8,128)(2,1)}, u32[]{:S(2)}, u32[]{:S(2)}) collective-permute-start(bf16[2048,256]{1,0:T(8,128)(2,1)} %collective-permute-done.8.refs_2_), channel_id=1, source_target_pairs={{0,1},{1,0},{2,3},{3,2},{4,5},{5,4},{6,7},{7,6},{8,9},{9,8},{10,11... | collective-permute-start | bytes 3145736 | tf_op jit(solution)/shard_map/ppermute | solution.py:709
  52.1 12.2 %collective-permute-start.13 = (bf16[2048,256]{1,0:T(8,128)(2,1)}, bf16[2048,256]{1,0:T(8,128)(2,1)S(1)}, u32[]{:S(2)}, u32[]{:S(2)}) collective-permute-start(bf16[2048,256]{1,0:T(8,128)(2,1)} %copy-done.7), channel_id=1, source_target_pairs={{0,1},{1,0},{2,3},{3,2},{4,5},{5,4},{6,7},{7,6},{8,9},{9,8},{10,11... | collective-permute-start | bytes 3145736 | tf_op jit(solution)/shard_map/ppermute | solution.py:709
  60.3 4.0 %collective-permute-start.15 = (bf16[2048,256]{1,0:T(8,128)(2,1)}, bf16[2048,256]{1,0:T(8,128)(2,1)S(1)}, u32[]{:S(2)}, u32[]{:S(2)}) collective-permute-start(bf16[2048,256]{1,0:T(8,128)(2,1)} %collective-permute-done.14.refs_6_), channel_id=1, source_target_pairs={{0,1},{1,0},{2,3},{3,2},{4,5},{5,4},{6,7},{7,6},{8,9},{9,8},{10,11... | collective-permute-start | bytes 3145736 | tf_op jit(solution)/shard_map/ppermute | solution.py:709
  60.3 37.4 %copy-start.1 = (s32[2]{0:T(128)S(1)}, s32[2]{0:T(128)}, u32[]{:S(2)}) copy-start(s32[2]{0:T(128)} %pad_add_fusion.here) | copy-start | bytes 28
  60.3 19.1 %collective-permute-start.16 = (bf16[2048,128]{1,0:T(8,128)(2,1)}, bf16[2048,128]{1,0:T(8,128)(2,1)S(1)}, u32[]{:S(2)}, u32[]{:S(2)}) collective-permute-start(bf16[2048,128]{1,0:T(8,128)(2,1)} %get-tuple-element.570), channel_id=1, source_target_pairs={{0,8},{24,16},{1,9},{25,17},{2,10},{26,18},{3,11},{27,19},{4,12},{... | collective-permute-start | bytes 1572872 | tf_op jit(solution)/shard_map/ppermute | solution.py:726
  64.3 15.0 %copy-start.8 = (bf16[2048,256]{1,0:T(8,128)(2,1)}, bf16[2048,256]{1,0:T(8,128)(2,1)S(1)}, u32[]{:S(2)}) copy-start(bf16[2048,256]{1,0:T(8,128)(2,1)S(1)} %collective-permute-done.13.refs_5_) | copy-start | bytes 3145732
  64.3 0.6 copy-start
  65.0 0.6 copy-start.2
  65.6 13.7 %copy-start.9 = (bf16[2048,256]{1,0:T(8,128)(2,1)}, bf16[2048,256]{1,0:T(8,128)(2,1)S(1)}, u32[]{:S(2)}) copy-start(bf16[2048,256]{1,0:T(8,128)(2,1)S(1)} %collective-permute-done.15.refs_7_) | copy-start | bytes 3145732
  79.3 9.7 %copy-start.5 = (bf16[2048,128]{1,0:T(8,128)(2,1)}, bf16[2048,128]{1,0:T(8,128)(2,1)S(1)}, u32[]{:S(2)}) copy-start(bf16[2048,128]{1,0:T(8,128)(2,1)S(1)} %collective-permute-done.16) | copy-start | bytes 1572868
  87.7 22.6 %collective-permute-start.20 = (bf16[3088,128]{1,0:T(8,128)(2,1)S(1)}, bf16[3088,128]{1,0:T(8,128)(2,1)}, u32[]{:S(2)}, u32[]{:S(2)}) collective-permute-start(bf16[3088,128]{1,0:T(8,128)(2,1)S(1)} %get-tuple-element.566), channel_id=1, source_target_pairs={{16,24},{8,0},{17,25},{9,1},{18,26},{10,2},{19,27},{11,3},{20,28},... | collective-permute-start | bytes 2371592 | tf_op jit(solution)/shard_map/ppermute | solution.py:731
  100.0 25.5 %collective-permute-start.19 = (bf16[3088,128]{1,0:T(8,128)(2,1)S(1)}, bf16[3088,128]{1,0:T(8,128)(2,1)}, u32[]{:S(2)}, u32[]{:S(2)}) collective-permute-start(bf16[3088,128]{1,0:T(8,128)(2,1)S(1)} %choose.1), channel_id=1, source_target_pairs={{16,24},{8,0},{17,25},{9,1},{18,26},{10,2},{19,27},{11,3},{20,28},... | collective-permute-start | bytes 2371592 | tf_op jit(solution)/shard_map/ppermute | solution.py:733
  101.3 26.8 %collective-permute-start.21 = (bf16[2048,128]{1,0:T(8,128)(2,1)}, bf16[2048,128]{1,0:T(8,128)(2,1)}, u32[]{:S(2)}, u32[]{:S(2)}) collective-permute-start(bf16[2048,128]{1,0:T(8,128)(2,1)} %get-tuple-element.570), channel_id=1, source_target_pairs={{0,16},{24,8},{1,17},{25,9},{2,18},{26,10},{3,19},{27,11},{4,20},{... | collective-permute-start | bytes 1572872 | tf_op jit(solution)/shard_map/ppermute | solution.py:726
  106.6 21.5 %collective-permute-start.22 = (bf16[2048,128]{1,0:T(8,128)(2,1)}, bf16[2048,128]{1,0:T(8,128)(2,1)}, u32[]{:S(2)}, u32[]{:S(2)}) collective-permute-start(bf16[2048,128]{1,0:T(8,128)(2,1)} %get-tuple-element.570), channel_id=1, source_target_pairs={{8,16},{16,8},{9,17},{17,9},{10,18},{18,10},{11,19},{19,11},{12,20... | collective-permute-start | bytes 1572872 | tf_op jit(solution)/shard_map/ppermute | solution.py:726
  115.2 12.9 %copy-start.4 = (bf16[2048,128]{1,0:T(8,128)(2,1)S(1)}, bf16[2048,128]{1,0:T(8,128)(2,1)}, u32[]{:S(2)}) copy-start(bf16[2048,128]{1,0:T(8,128)(2,1)} %get-tuple-element.570) | copy-start | bytes 1572868
  115.2 12.9 %copy-start.6 = (bf16[2048,128]{1,0:T(8,128)(2,1)S(1)}, bf16[2048,128]{1,0:T(8,128)(2,1)}, u32[]{:S(2)}) copy-start(bf16[2048,128]{1,0:T(8,128)(2,1)} %copy-done.5) | copy-start | bytes 1572868
  129.6 17.8 %collective-permute-start.2 = (bf16[1536,128]{1,0:T(8,128)(2,1)S(1)}, bf16[1536,128]{1,0:T(8,128)(2,1)S(1)}, u32[]{:S(2)}, u32[]{:S(2)}) collective-permute-start(bf16[1536,128]{1,0:T(8,128)(2,1)S(1)} %pool.9), channel_id=1, source_target_pairs={{16,24},{8,0},{17,25},{9,1},{18,26},{10,2},{19,27},{11,3},{20,28},... | collective-permute-start | bytes 1179656 | tf_op jit(solution)/shard_map/cond/branch_2_fun/ppermute | solution.py:685

commit v4 on v3

--- a/solution.py
+++ b/solution.py
@@ -349,12 +349,14 @@
     )(info, lf, *spread)
 
 
-def out_copy(out, held, sem, slot, pair):
+def out_copy(out, held, sem, slot, pair, r):
+    half = held.shape[1] // 2
+    at = pl.ds(pl.multiple_of(r * half, half), half)
     if len(out.shape) == 3:
-        return pltpu.make_async_copy(held.at[slot], out.at[pair], sem.at[slot])
-    return pltpu.make_async_copy(
-        held.at[slot], out.at[:, pl.ds(pl.multiple_of(pair * PAIR, PAIR), PAIR)], sem.at[slot]
-    )
+        to = out.at[pair, at, :]
+    else:
+        to = out.at[at, pl.ds(pl.multiple_of(pair * PAIR, PAIR), PAIR)]
+    return pltpu.make_async_copy(held.at[slot, at, :], to, sem.at[slot, r])
 
 
 def t2_copies(act, col, part, t2, t2_v, sem, rs=(0, 1)):
@@ -383,7 +385,7 @@
     half = held.shape[1] // 2
 
     def acc_copy(pair, slot):
-        return pltpu.make_async_copy(acc.at[pair], acc_v.at[slot], acc_sem.at[slot])
+        return pltpu.make_async_copy(acc.at[pair], acc_v.at[slot], acc_sem.at[slot, 0])
 
     if acc is not None:
 
@@ -409,7 +411,8 @@
 
         @pl.when(pair >= lo + 2)
         def _():
-            out_copy(out, held, sem, slot, pair).wait()
+            for r in range(2):
+                out_copy(out, held, sem, slot, pair, r).wait()
 
         @pl.loop(0, 2)
         def _(r):
@@ -422,14 +425,14 @@
             if acc is not None:
                 product = product + acc_v[slot, at, :]
             held[slot, at, :] = product.astype(held.dtype)
-
-        out_copy(out, held, sem, slot, pair).start()
+            out_copy(out, held, sem, slot, pair, r).start()
 
     for back in (1, 2):
 
         @pl.when(hi - back >= lo)
         def _():
-            out_copy(out, held, sem, lax.rem(hi - back - lo, 2), 0).wait()
+            for r in range(2):
+                out_copy(out, held, sem, lax.rem(hi - back - lo, 2), 0, r).wait()
 
 
 def main_kernel(sz, chunks, n_t2, info, place, *refs):
@@ -558,7 +561,7 @@
             pltpu.VMEM((2, ij, PAIR), jnp.float32),
             pltpu.VMEM((ij, cd), BF16),
             pltpu.SemaphoreType.DMA((sz.near,)),
-            pltpu.SemaphoreType.DMA((2,)),
+            pltpu.SemaphoreType.DMA((2, 2)),
             pltpu.SemaphoreType.DMA((len(t2), 2)),
         ],
         compiler_params=PARAMS,
@@ -591,8 +594,8 @@
             pltpu.VMEM((2, ij, PAIR), jnp.float32),
             *([pltpu.VMEM((ij, cd), BF16)] if chunks == 1 else []),
             pltpu.SemaphoreType.DMA((sz.n, 3)),
-            pltpu.SemaphoreType.DMA((2,)),
-            pltpu.SemaphoreType.DMA((2,)),
+            pltpu.SemaphoreType.DMA((2, 2)),
+            pltpu.SemaphoreType.DMA((2, 2)),
             pltpu.SemaphoreType.DMA((len(t2), 2)),
         ],
         input_output_aliases=aliases,
@@ -671,7 +674,7 @@
             pltpu.VMEM((region, TILE), BF16),
             pltpu.VMEM((2, ij, PAIR), BF16),
             pltpu.SemaphoreType.DMA((sz.n - 1,)),
-            pltpu.SemaphoreType.DMA((2,)),
+            pltpu.SemaphoreType.DMA((2, 2)),
         ],
         input_output_aliases={2: 0},
         compiler_params=PARAMS,

time: 156 us -> 155 us (level)
  no operation moved by 1% of the time
where the time goes in v4:
time: 155 us; the launch traced here: 152 us
  Pallas kernels  61.9 us (40%)
  waiting for transfers between devices  45.6 us (29%)
  starting transfers between devices  30.1 us (19%)
  blocking collectives  8.63 us (6%)
  local copies, waits for them, and re-layouts  2.49 us (2%)
  between operations  1.86 us (1%)
    ppermute x7, waiting for transfers between devices, across(): return lax.ppermute(value, 'col', [(i, i ^ d) for i in range(n_col)])  29.6 us
    pallas_call x2, Pallas kernels, main_part(): pl.pallas_call(functools.partial(main_kernel, sz, chunks, len(t2)), out_s...  26.1 us
    ppermute x4, waiting for transfers between devices, hop(): return (lax.ppermute(up, 'row', pairs), lax.ppermute(down, 'row', back))  13.8 us
    pallas_call x1, Pallas kernels, early_part(): pl.pallas_call(functools.partial(early_kernel, sz, len(t2)), out_shape=pl...  13.4 us
    ppermute x3, starting transfers between devices, leftovers(): return lax.ppermute(tie(lf, after), 'row', pairs)  10.7 us
    ppermute x4, starting transfers between devices, hop(): return (lax.ppermute(up, 'row', pairs), lax.ppermute(down, 'row', back))  9.4 us
    pmax x1, blocking collectives, body(): need = lax.pmax(need, 'col')  8.63 us
    ppermute x7, starting transfers between devices, across(): return lax.ppermute(value, 'col', [(i, i ^ d) for i in range(n_col)])  6.15 us
  transfers between devices with their start and end apart: 17, of which 6 were waited for; matrix products, arithmetic and copies ran while one was open for 1% of the time, Pallas kernels for 33%

profile of v4, /device:TPU:0, one launch (start us, length us, event | category | flops | bytes accessed | tf_op | source)
XLA Modules:
  0.0 152.0 jit_solution(16365537346580447678)
XLA Ops:
  0.0 4.0 %begin.1 = (bf16[6160,128]{1,0:T(8,128)(2,1)S(1)}, bf16[2048,128]{1,0:T(8,128)(2,1)}, bf16[2048,256]{1,0:T(8,128)(2,1)}) custom-call(s32[4,16]{1,0:T(4,128)} %v_mask_hbm.1, s32[4,16]{1,0:T(4,128)} %v_mask_hbm.1, s32[2,16]{1,0:T(2,128)} %bitcast.6, bf16[512,2048]{1,0:T(8,128)(2,1)} %v.1, bf16[2048,256]{1,0:T(8,128)(2,1)} %t2.1), custom_call_target="tpu_custom_call" | custom-call | tf_op jit(solution)/shard_map/begin/pallas_call | solution.py:93
  4.0 5.0 %collective-permute-start.11 = (bf16[6160,128]{1,0:T(8,128)(2,1)S(1)}, bf16[6160,128]{1,0:T(8,128)(2,1)S(1)}, u32[]{:S(2)}, u32[]{:S(2)}) collective-permute-start(bf16[6160,128]{1,0:T(8,128)(2,1)S(1)} %get-tuple-element.556.own.refs_8_.refs_0_), channel_id=1, source_target_pairs={{0,8},{8,16},{16,24},{1,9},{9,17},{17,25},{2,10},{10,18},{18,26},{... | collective-permute-start | bytes 4730888 | tf_op jit(solution)/shard_map/ppermute | solution.py:709
  9.0 1.3 collective-permute-start.12
  10.3 1.6 %collective-permute-start.8 = (bf16[2048,256]{1,0:T(8,128)(2,1)}, bf16[2048,256]{1,0:T(8,128)(2,1)}, u32[]{:S(2)}, u32[]{:S(2)}) collective-permute-start(bf16[2048,256]{1,0:T(8,128)(2,1)} %get-tuple-element.558.refs_0_), channel_id=1, source_target_pairs={{0,2},{1,3},{2,0},{3,1},{4,6},{5,7},{6,4},{7,5},{8,10},{9,11},{10,... | collective-permute-start | bytes 3145736 | tf_op jit(solution)/shard_map/ppermute | solution.py:712
  11.9 1.5 collective-permute-start.10
  13.4 21.9 %collective-permute-done.8.refs_2_ = bf16[2048,256]{1,0:T(8,128)(2,1)} collective-permute-done((bf16[2048,256]{1,0:T(8,128)(2,1)}, bf16[2048,256]{1,0:T(8,128)(2,1)}, u32[]{:S(2)}, u32[]{:S(2)}) %collective-permute-start.8) | collective-permute-done | bytes 1048608 | tf_op jit(solution)/shard_map/ppermute | solution.py:712
  35.3 2.4 %collective-permute-start.14 = (bf16[2048,256]{1,0:T(8,128)(2,1)}, bf16[2048,256]{1,0:T(8,128)(2,1)}, u32[]{:S(2)}, u32[]{:S(2)}) collective-permute-start(bf16[2048,256]{1,0:T(8,128)(2,1)} %get-tuple-element.558.refs_0_), channel_id=1, source_target_pairs={{0,6},{1,7},{2,4},{3,5},{4,2},{5,3},{6,0},{7,1},{8,14},{9,15},{10,... | collective-permute-start | bytes 3145736 | tf_op jit(solution)/shard_map/ppermute | solution.py:712
  37.8 4.9 %collective-permute-done.11.refs_0_.refs_9_.refs_1_ = bf16[6160,128]{1,0:T(8,128)(2,1)S(1)} collective-permute-done((bf16[6160,128]{1,0:T(8,128)(2,1)S(1)}, bf16[6160,128]{1,0:T(8,128)(2,1)S(1)}, u32[]{:S(2)}, u32[]{:S(2)}) %collective-permute-start.11) | collective-permute-done | bytes 1576992 | tf_op jit(solution)/shard_map/ppermute | solution.py:709
  42.7 1.8 %collective-permute-start.17 = (bf16[6160,128]{1,0:T(8,128)(2,1)S(1)}, bf16[6160,128]{1,0:T(8,128)(2,1)}, u32[]{:S(2)}, u32[]{:S(2)}) collective-permute-start(bf16[6160,128]{1,0:T(8,128)(2,1)S(1)} %collective-permute-done.11.refs_0_.refs_9_.refs_1_), channel_id=1, source_target_pairs={{8,16},{16,24},{9,17},{17,25},{10,18},{18,26},{11,19},{19,27},{12,... | collective-permute-start | bytes 4730888 | tf_op jit(solution)/shard_map/ppermute | solution.py:709
  44.5 2.5 %collective-permute-done.12.refs_1_.refs_10_.refs_2_ = bf16[6160,128]{1,0:T(8,128)(2,1)} collective-permute-done((bf16[6160,128]{1,0:T(8,128)(2,1)S(1)}, bf16[6160,128]{1,0:T(8,128)(2,1)}, u32[]{:S(2)}, u32[]{:S(2)}) %collective-permute-start.12) | collective-permute-done | bytes 1576992 | tf_op jit(solution)/shard_map/ppermute | solution.py:709
  47.0 1.3 collective-permute-start.18
  49.0 3.1 %near_plan.1.place = s32[96]{0:T(128)} custom-call(s32[2]{0:T(128)} %pad_add_fusion.here, bf16[6160,128]{1,0:T(8,128)(2,1)S(1)} %get-tuple-element.556.own.refs_8_.refs_0_, bf16[6160,128]{1,0:T(8,128)(2,1)S(1)} %collective-permute-done.11.refs_0_.refs_9_.refs_1_, bf16[6160,128]{1,0:T(8,128)(2,1)} %collective-permute-done.12.refs_1_.refs_10_.refs_2_), custom_call_target="tpu_custom_call" | custom-call | tf_op jit(solution)/shard_map/near_plan/pallas_call | solution.py:184
  52.6 7.7 %collective-permute-done.14.refs_6_ = bf16[2048,256]{1,0:T(8,128)(2,1)} collective-permute-done((bf16[2048,256]{1,0:T(8,128)(2,1)}, bf16[2048,256]{1,0:T(8,128)(2,1)}, u32[]{:S(2)}, u32[]{:S(2)}) %collective-permute-start.14) | collective-permute-done | bytes 1048608 | tf_op jit(solution)/shard_map/ppermute | solution.py:712
  60.3 4.0 %collective-permute-start.16 = (bf16[2048,128]{1,0:T(8,128)(2,1)}, bf16[2048,128]{1,0:T(8,128)(2,1)S(1)}, u32[]{:S(2)}, u32[]{:S(2)}) collective-permute-start(bf16[2048,128]{1,0:T(8,128)(2,1)} %get-tuple-element.570), channel_id=1, source_target_pairs={{0,8},{24,16},{1,9},{25,17},{2,10},{26,18},{3,11},{27,19},{4,12},{... | collective-permute-start | bytes 1572872 | tf_op jit(solution)/shard_map/ppermute | solution.py:729
  65.6 13.4 %early_part.1.refs_14_ = f32[6,2048,256]{2,1,0:T(8,128)} custom-call(s32[2]{0:T(128)S(1)} %copy-done, s32[96]{0:T(128)S(1)} %copy-done.2, bf16[2048,256]{1,0:T(8,128)(2,1)} %get-tuple-element.558.refs_0_, bf16[2048,256]{1,0:T(8,128)(2,1)} %collective-permute-done.7.refs_1_, bf16[2048,256]{1,0:T(8,128)(2,1)} %collective-permute-done.8.refs_2_, ...), custom_call_target="tpu_custom_call" | custom-call | flops 1048576 | bytes 4096 | tf_op jit(solution)/shard_map/early_part/pallas_call | solution.py:553
  79.0 6.4 %collective-permute-done.18.refs_4_.down.refs_12_ = bf16[6160,128]{1,0:T(8,128)(2,1)} collective-permute-done((bf16[6160,128]{1,0:T(8,128)(2,1)}, bf16[6160,128]{1,0:T(8,128)(2,1)}, u32[]{:S(2)}, u32[]{:S(2)}) %collective-permute-start.18) | collective-permute-done | bytes 1576992 | tf_op jit(solution)/shard_map/ppermute | solution.py:709
  85.4 2.3 %choose_first.1 = (bf16[3088,128]{1,0:T(8,128)(2,1)S(1)}, s32[1]{0:T(128)}) custom-call(s32[2]{0:T(128)S(1)} %copy-done, bf16[6160,128]{1,0:T(8,128)(2,1)S(1)} %get-tuple-element.556.own.refs_8_.refs_0_, bf16[6160,128]{1,0:T(8,128)(2,1)} %copy-done.3, bf16[6160,128]{1,0:T(8,128)(2,1)} %collective-permute-done.12.refs_1_.refs_10_.refs_2_, ...), custom_call_target="tpu_custom_call" | custom-call | tf_op jit(solution)/shard_map/choose_first/pallas_call | solution.py:307
  87.7 1.3 collective-permute-start.20
  89.0 8.6 %pmax.7.need = s32[1]{0:T(128)} all-reduce(s32[1]{0:T(128)} %get-tuple-element.564), channel_id=1, replica_groups=mesh['row'=4,'col'=8] {'col'}, use_global_device_ids=true, to_apply=%region_0.0 | all-reduce | flops 1 | bytes 8 | tf_op jit(solution)/shard_map/pmax | solution.py:735
  97.6 2.4 %choose.1 = bf16[3088,128]{1,0:T(8,128)(2,1)S(1)} custom-call(s32[2]{0:T(128)S(1)} %copy-done.1, s32[1]{0:T(128)} %pmax.7.need, bf16[6160,128]{1,0:T(8,128)(2,1)} %collective-permute-done.17.refs_3_.up.refs_11_, bf16[6160,128]{1,0:T(8,128)(2,1)} %collective-permute-done.18.refs_4_.down.refs_12_), custom_call_target="tpu_custom_call" | custom-call | tf_op jit(solution)/shard_map/choose/pallas_call | solution.py:283
  100.0 1.3 collective-permute-start.19
  101.3 5.2 %collective-permute-start.21 = (bf16[2048,128]{1,0:T(8,128)(2,1)}, bf16[2048,128]{1,0:T(8,128)(2,1)}, u32[]{:S(2)}, u32[]{:S(2)}) collective-permute-start(bf16[2048,128]{1,0:T(8,128)(2,1)} %get-tuple-element.570), channel_id=1, source_target_pairs={{0,16},{24,8},{1,17},{25,9},{2,18},{26,10},{3,19},{27,11},{4,20},{... | collective-permute-start | bytes 1572872 | tf_op jit(solution)/shard_map/ppermute | solution.py:729
  106.6 1.5 collective-permute-start.22
  108.0 2.2 %collective-permute-done.20.refs_5_.refs_13_ = bf16[3088,128]{1,0:T(8,128)(2,1)} collective-permute-done((bf16[3088,128]{1,0:T(8,128)(2,1)S(1)}, bf16[3088,128]{1,0:T(8,128)(2,1)}, u32[]{:S(2)}, u32[]{:S(2)}) %collective-permute-start.20) | collective-permute-done | bytes 790560 | tf_op jit(solution)/shard_map/ppermute | solution.py:734
  110.3 4.9 %plan.1 = (s32[256]{0:T(256)S(1)}, s32[256]{0:T(256)S(1)}, s32[10]{0:T(128)S(1)}) custom-call(s32[2]{0:T(128)} %pad_add_fusion.here, bf16[6160,128]{1,0:T(8,128)(2,1)S(1)} %get-tuple-element.556.own.refs_8_.refs_0_, bf16[6160,128]{1,0:T(8,128)(2,1)} %copy-done.3, bf16[6160,128]{1,0:T(8,128)(2,1)} %collective-permute-done.12.refs_1_.refs_10_.refs_2_, ...), custom_call_target="tpu_custom_call" | custom-call | tf_op jit(solution)/shard_map/plan/pallas_call | solution.py:248
  115.2 11.7 %main_part.15 = bf16[2048,2048]{1,0:T(8,128)(2,1)} custom-call(s32[10]{0:T(128)S(1)} %get-tuple-element.567.info, s32[256]{0:T(256)S(1)} %get-tuple-element.568.place, bf16[2048,256]{1,0:T(8,128)(2,1)} %get-tuple-element.558.refs_0_, bf16[2048,256]{1,0:T(8,128)(2,1)} %collective-permute-done.7.refs_1_, bf16[2048,256]{1,0:T(8,128)(2,1)} %collective-permute-done.8.refs_2_, ...), custom_call_target="tpu_custom_call" | custom-call | flops 1048576 | bytes 4096 | tf_op jit(solution)/shard_map/main_part/pallas_call | solution.py:585
  126.9 1.2 slice.3
  129.5 22.2 %conditional.1 = (bf16[2048,2048]{1,0:T(8,128)(2,1)}) conditional(s32[]{:T(128)} %clamp.3, (s32[10]{0:T(128)S(1)}, s32[256]{0:T(256)S(1)}, bf16[2048,256]{1,0:T(8,128)(2,1)}, bf16[2048,256]{1,0:T(8,128)(2,1)}, bf16[2048,256]{1,0:T(8,128)(2,1)}, /*index=5*/bf16[2048,256]{1,0:T(8,128)(2,1)}, ...), branch_computations={%region_1.2_spmd, %region_2.3_spmd, %region_3.4_spmd, %region_4.5_... | conditional | flops 2097152 | bytes 6299696 | solution.py:745
  129.5 1.2 pool.8
  130.8 1.3 collective-permute-start.1
  132.1 14.5 %main_part.9 = (bf16[2048,2048]{1,0:T(8,128)(2,1)}, bf16[2,2048,256]{2,1,0:T(8,128)(2,1)S(1)}, bf16[2048,2048]{1,0:T(8,128)(2,1)S(1)}) custom-call(s32[10]{0:T(128)S(1)} %get-tuple-element.376.info, s32[256]{0:T(256)S(1)} %get-tuple-element.378.place, bf16[2048,256]{1,0:T(8,128)(2,1)} %get-tuple-element.379.refs_0_, ...), custom_call_target="tpu_custom_call", output_to_operand_aliasing={{0}: (19, {})} | custom-call | flops 1048576 | bytes 4096 | tf_op jit(solution)/shard_map/cond/branch_1_fun/main_part/pallas_call | solution.py:585
  146.5 4.5 %tail_part.8 = bf16[2048,2048]{1,0:T(8,128)(2,1)} custom-call(s32[10]{0:T(128)S(1)} %get-tuple-element.376.info, s32[256]{0:T(256)S(1)} %get-tuple-element.377.late, bf16[2048,2048]{1,0:T(8,128)(2,1)} %get-tuple-element.397.begun, bf16[2,2048,256]{2,1,0:T(8,128)(2,1)S(1)} %get-tuple-element.398.rest, ...), custom_call_target="tpu_custom_call", output_to_operand_aliasing={{}: (2, {})} | custom-call | flops 1048576 | bytes 4096 | tf_op jit(solution)/shard_map/cond/branch_1_fun/tail_part/pallas_call | solution.py:667
  (36 shorter events, 2.5 us)
Async XLA Ops:
  4.0 38.7 %collective-permute-start.11 = (bf16[6160,128]{1,0:T(8,128)(2,1)S(1)}, bf16[6160,128]{1,0:T(8,128)(2,1)S(1)}, u32[]{:S(2)}, u32[]{:S(2)}) collective-permute-start(bf16[6160,128]{1,0:T(8,128)(2,1)S(1)} %get-tuple-element.556.own.refs_8_.refs_0_), channel_id=1, source_target_pairs={{0,8},{8,16},{16,24},{1,9},{9,17},{17,25},{2,10},{10,18},{18,26},{... | collective-permute-start | bytes 4730888 | tf_op jit(solution)/shard_map/ppermute | solution.py:709
  9.0 37.9 %collective-permute-start.12 = (bf16[6160,128]{1,0:T(8,128)(2,1)S(1)}, bf16[6160,128]{1,0:T(8,128)(2,1)}, u32[]{:S(2)}, u32[]{:S(2)}) collective-permute-start(bf16[6160,128]{1,0:T(8,128)(2,1)S(1)} %get-tuple-element.556.own.refs_8_.refs_0_), channel_id=1, source_target_pairs={{24,16},{16,8},{8,0},{25,17},{17,9},{9,1},{26,18},{18,10},{10,2},{... | collective-permute-start | bytes 4730888 | tf_op jit(solution)/shard_map/ppermute | solution.py:709
  10.3 25.0 %collective-permute-start.8 = (bf16[2048,256]{1,0:T(8,128)(2,1)}, bf16[2048,256]{1,0:T(8,128)(2,1)}, u32[]{:S(2)}, u32[]{:S(2)}) collective-permute-start(bf16[2048,256]{1,0:T(8,128)(2,1)} %get-tuple-element.558.refs_0_), channel_id=1, source_target_pairs={{0,2},{1,3},{2,0},{3,1},{4,6},{5,7},{6,4},{7,5},{8,10},{9,11},{10,... | collective-permute-start | bytes 3145736 | tf_op jit(solution)/shard_map/ppermute | solution.py:712
  11.9 25.9 %collective-permute-start.10 = (bf16[2048,256]{1,0:T(8,128)(2,1)}, bf16[2048,256]{1,0:T(8,128)(2,1)S(1)}, u32[]{:S(2)}, u32[]{:S(2)}) collective-permute-start(bf16[2048,256]{1,0:T(8,128)(2,1)} %get-tuple-element.558.refs_0_), channel_id=1, source_target_pairs={{0,4},{1,5},{2,6},{3,7},{4,0},{5,1},{6,2},{7,3},{8,12},{9,13},{10,... | collective-permute-start | bytes 3145736 | tf_op jit(solution)/shard_map/ppermute | solution.py:712
  13.4 38.6 %collective-permute-start.7 = (bf16[2048,256]{1,0:T(8,128)(2,1)}, bf16[2048,256]{1,0:T(8,128)(2,1)}, u32[]{:S(2)}, u32[]{:S(2)}) collective-permute-start(bf16[2048,256]{1,0:T(8,128)(2,1)} %get-tuple-element.558.refs_0_), channel_id=1, source_target_pairs={{0,1},{1,0},{2,3},{3,2},{4,5},{5,4},{6,7},{7,6},{8,9},{9,8},{10,11... | collective-permute-start | bytes 3145736 | tf_op jit(solution)/shard_map/ppermute | solution.py:712
  35.3 24.9 %collective-permute-start.14 = (bf16[2048,256]{1,0:T(8,128)(2,1)}, bf16[2048,256]{1,0:T(8,128)(2,1)}, u32[]{:S(2)}, u32[]{:S(2)}) collective-permute-start(bf16[2048,256]{1,0:T(8,128)(2,1)} %get-tuple-element.558.refs_0_), channel_id=1, source_target_pairs={{0,6},{1,7},{2,4},{3,5},{4,2},{5,3},{6,0},{7,1},{8,14},{9,15},{10,... | collective-permute-start | bytes 3145736 | tf_op jit(solution)/shard_map/ppermute | solution.py:712
  37.8 9.2 %copy-start.7 = (bf16[2048,256]{1,0:T(8,128)(2,1)}, bf16[2048,256]{1,0:T(8,128)(2,1)S(1)}, u32[]{:S(2)}) copy-start(bf16[2048,256]{1,0:T(8,128)(2,1)S(1)} %collective-permute-done.10.refs_4_) | copy-start | bytes 3145732
  42.7 36.3 %copy-start.3 = (bf16[6160,128]{1,0:T(8,128)(2,1)}, bf16[6160,128]{1,0:T(8,128)(2,1)S(1)}, u32[]{:S(2)}) copy-start(bf16[6160,128]{1,0:T(8,128)(2,1)S(1)} %collective-permute-done.11.refs_0_.refs_9_.refs_1_) | copy-start | bytes 4730884
  42.7 36.3 %collective-permute-start.17 = (bf16[6160,128]{1,0:T(8,128)(2,1)S(1)}, bf16[6160,128]{1,0:T(8,128)(2,1)}, u32[]{:S(2)}, u32[]{:S(2)}) collective-permute-start(bf16[6160,128]{1,0:T(8,128)(2,1)S(1)} %collective-permute-done.11.refs_0_.refs_9_.refs_1_), channel_id=1, source_target_pairs={{8,16},{16,24},{9,17},{17,25},{10,18},{18,26},{11,19},{19,27},{12,... | collective-permute-start | bytes 4730888 | tf_op jit(solution)/shard_map/ppermute | solution.py:709
  47.0 38.4 %collective-permute-start.18 = (bf16[6160,128]{1,0:T(8,128)(2,1)}, bf16[6160,128]{1,0:T(8,128)(2,1)}, u32[]{:S(2)}, u32[]{:S(2)}) collective-permute-start(bf16[6160,128]{1,0:T(8,128)(2,1)} %collective-permute-done.12.refs_1_.refs_10_.refs_2_), channel_id=1, source_target_pairs={{16,8},{8,0},{17,9},{9,1},{18,10},{10,2},{19,11},{11,3},{20,12},{1... | collective-permute-start | bytes 4730888 | tf_op jit(solution)/shard_map/ppermute | solution.py:709
  48.3 12.0 %collective-permute-start.9 = (bf16[2048,256]{1,0:T(8,128)(2,1)}, bf16[2048,256]{1,0:T(8,128)(2,1)}, u32[]{:S(2)}, u32[]{:S(2)}) collective-permute-start(bf16[2048,256]{1,0:T(8,128)(2,1)} %collective-permute-done.8.refs_2_), channel_id=1, source_target_pairs={{0,1},{1,0},{2,3},{3,2},{4,5},{5,4},{6,7},{7,6},{8,9},{9,8},{10,11... | collective-permute-start | bytes 3145736 | tf_op jit(solution)/shard_map/ppermute | solution.py:712
  52.1 12.2 %collective-permute-start.13 = (bf16[2048,256]{1,0:T(8,128)(2,1)}, bf16[2048,256]{1,0:T(8,128)(2,1)S(1)}, u32[]{:S(2)}, u32[]{:S(2)}) collective-permute-start(bf16[2048,256]{1,0:T(8,128)(2,1)} %copy-done.7), channel_id=1, source_target_pairs={{0,1},{1,0},{2,3},{3,2},{4,5},{5,4},{6,7},{7,6},{8,9},{9,8},{10,11... | collective-permute-start | bytes 3145736 | tf_op jit(solution)/shard_map/ppermute | solution.py:712
  60.3 4.0 %collective-permute-start.15 = (bf16[2048,256]{1,0:T(8,128)(2,1)}, bf16[2048,256]{1,0:T(8,128)(2,1)S(1)}, u32[]{:S(2)}, u32[]{:S(2)}) collective-permute-start(bf16[2048,256]{1,0:T(8,128)(2,1)} %collective-permute-done.14.refs_6_), channel_id=1, source_target_pairs={{0,1},{1,0},{2,3},{3,2},{4,5},{5,4},{6,7},{7,6},{8,9},{9,8},{10,11... | collective-permute-start | bytes 3145736 | tf_op jit(solution)/shard_map/ppermute | solution.py:712
  60.3 37.4 %copy-start.1 = (s32[2]{0:T(128)S(1)}, s32[2]{0:T(128)}, u32[]{:S(2)}) copy-start(s32[2]{0:T(128)} %pad_add_fusion.here) | copy-start | bytes 28
  60.3 18.7 %collective-permute-start.16 = (bf16[2048,128]{1,0:T(8,128)(2,1)}, bf16[2048,128]{1,0:T(8,128)(2,1)S(1)}, u32[]{:S(2)}, u32[]{:S(2)}) collective-permute-start(bf16[2048,128]{1,0:T(8,128)(2,1)} %get-tuple-element.570), channel_id=1, source_target_pairs={{0,8},{24,16},{1,9},{25,17},{2,10},{26,18},{3,11},{27,19},{4,12},{... | collective-permute-start | bytes 1572872 | tf_op jit(solution)/shard_map/ppermute | solution.py:729
  64.3 14.7 %copy-start.8 = (bf16[2048,256]{1,0:T(8,128)(2,1)}, bf16[2048,256]{1,0:T(8,128)(2,1)S(1)}, u32[]{:S(2)}) copy-start(bf16[2048,256]{1,0:T(8,128)(2,1)S(1)} %collective-permute-done.13.refs_5_) | copy-start | bytes 3145732
  64.3 0.6 copy-start
  65.0 0.6 copy-start.2
  65.6 13.4 %copy-start.9 = (bf16[2048,256]{1,0:T(8,128)(2,1)}, bf16[2048,256]{1,0:T(8,128)(2,1)S(1)}, u32[]{:S(2)}) copy-start(bf16[2048,256]{1,0:T(8,128)(2,1)S(1)} %collective-permute-done.15.refs_7_) | copy-start | bytes 3145732
  79.0 10.0 %copy-start.5 = (bf16[2048,128]{1,0:T(8,128)(2,1)}, bf16[2048,128]{1,0:T(8,128)(2,1)S(1)}, u32[]{:S(2)}) copy-start(bf16[2048,128]{1,0:T(8,128)(2,1)S(1)} %collective-permute-done.16) | copy-start | bytes 1572868
  87.7 22.6 %collective-permute-start.20 = (bf16[3088,128]{1,0:T(8,128)(2,1)S(1)}, bf16[3088,128]{1,0:T(8,128)(2,1)}, u32[]{:S(2)}, u32[]{:S(2)}) collective-permute-start(bf16[3088,128]{1,0:T(8,128)(2,1)S(1)} %get-tuple-element.566), channel_id=1, source_target_pairs={{16,24},{8,0},{17,25},{9,1},{18,26},{10,2},{19,27},{11,3},{20,28},... | collective-permute-start | bytes 2371592 | tf_op jit(solution)/shard_map/ppermute | solution.py:734
  100.0 26.9 %collective-permute-start.19 = (bf16[3088,128]{1,0:T(8,128)(2,1)S(1)}, bf16[3088,128]{1,0:T(8,128)(2,1)}, u32[]{:S(2)}, u32[]{:S(2)}) collective-permute-start(bf16[3088,128]{1,0:T(8,128)(2,1)S(1)} %choose.1), channel_id=1, source_target_pairs={{16,24},{8,0},{17,25},{9,1},{18,26},{10,2},{19,27},{11,3},{20,28},... | collective-permute-start | bytes 2371592 | tf_op jit(solution)/shard_map/ppermute | solution.py:736
  101.3 28.2 %collective-permute-start.21 = (bf16[2048,128]{1,0:T(8,128)(2,1)}, bf16[2048,128]{1,0:T(8,128)(2,1)}, u32[]{:S(2)}, u32[]{:S(2)}) collective-permute-start(bf16[2048,128]{1,0:T(8,128)(2,1)} %get-tuple-element.570), channel_id=1, source_target_pairs={{0,16},{24,8},{1,17},{25,9},{2,18},{26,10},{3,19},{27,11},{4,20},{... | collective-permute-start | bytes 1572872 | tf_op jit(solution)/shard_map/ppermute | solution.py:729
  106.6 22.9 %collective-permute-start.22 = (bf16[2048,128]{1,0:T(8,128)(2,1)}, bf16[2048,128]{1,0:T(8,128)(2,1)}, u32[]{:S(2)}, u32[]{:S(2)}) collective-permute-start(bf16[2048,128]{1,0:T(8,128)(2,1)} %get-tuple-element.570), channel_id=1, source_target_pairs={{8,16},{16,8},{9,17},{17,9},{10,18},{18,10},{11,19},{19,11},{12,20... | collective-permute-start | bytes 1572872 | tf_op jit(solution)/shard_map/ppermute | solution.py:729
  115.2 14.3 %copy-start.4 = (bf16[2048,128]{1,0:T(8,128)(2,1)S(1)}, bf16[2048,128]{1,0:T(8,128)(2,1)}, u32[]{:S(2)}) copy-start(bf16[2048,128]{1,0:T(8,128)(2,1)} %get-tuple-element.570) | copy-start | bytes 1572868
  115.2 14.3 %copy-start.6 = (bf16[2048,128]{1,0:T(8,128)(2,1)S(1)}, bf16[2048,128]{1,0:T(8,128)(2,1)}, u32[]{:S(2)}) copy-start(bf16[2048,128]{1,0:T(8,128)(2,1)} %copy-done.5) | copy-start | bytes 1572868
  130.8 15.8 %collective-permute-start.1 = (bf16[1280,128]{1,0:T(8,128)(2,1)S(1)}, bf16[1280,128]{1,0:T(8,128)(2,1)S(1)}, u32[]{:S(2)}, u32[]{:S(2)}) collective-permute-start(bf16[1280,128]{1,0:T(8,128)(2,1)S(1)} %pool.8), channel_id=1, source_target_pairs={{16,24},{8,0},{17,25},{9,1},{18,26},{10,2},{19,27},{11,3},{20,28},... | collective-permute-start | bytes 983048 | tf_op jit(solution)/shard_map/cond/branch_1_fun/ppermute | solution.py:688
